TPU v7x, 128 devices: a whole 4x4x4 slice. The times are simulated.
128 devices in a mesh: dp: 8 (over z_lo, y), section: 16 (over z_hi, x, core).
Axes of the slice: x: 4, y: 4, z: 4 (z_hi: 2, z_lo: 2; z = z_hi * 2 + z_lo), core: 2. Of those that a mesh axis runs over, the one named last changes fastest.
Arguments:
- layer_in: bfloat16 [16, 16, 64, 6144], P('section', None, 'dp'), may hold values from -6 to 6
- pre_act: bfloat16 [16, 16, 64, 6144], P('section', None, 'dp'), may hold values from -8 to 8
- weight: bfloat16 [16, 6144, 6144], P('section', 'dp'), may hold values from -1 to 1
- gain: float32 [16, 6144], P('section'), may hold values from 0.5 to 1.5
- cot_top: bfloat16 [16, 64, 6144], P(None, 'dp', 'section'), may hold values from -6 to 6
Outputs:
- cot_bottom: bfloat16 [16, 64, 6144], P(None, 'dp', 'section')
- weight_grad: bfloat16 [16, 6144, 6144], P('section', 'dp')
- gain_grad: float32 [16, 6144], P('section', 'dp')
All inputs are finite; a program needn't handle non-finite values.
Results may differ from a plain program's by a relative error of at most 0.035.
Values may be sent and summed in bfloat16 or wider, within the bound.
No kernel may reach another device: no remote copies, remote signals or barrier semaphores. Data moves between devices by JAX's collectives and lax.ppermute only.
A program may use at most 192 MiB of HBM per device.

v0:
```python
import jax
import jax.numpy as jnp
from jax import lax
from jax.sharding import PartitionSpec as P

norm_eps = 1e-05


def shifted(value, axis, steps):
    count = lax.axis_size(axis)
    leading, last = (max(0, -steps), min(count, count - steps))
    return lax.ppermute(value, axis, [(source, source + steps) for source in range(leading, last)])


def pass_down(out_grad):
    return shifted(out_grad, "section", -1)


def pick_slot(buffer, slot_clip):
    return lax.dynamic_index_in_dim(buffer, slot_clip, 0, keepdims=False)


def put_slot(buffer, new_value, slot_clip, is_live):
    old_value = pick_slot(buffer, slot_clip)
    return lax.dynamic_update_index_in_dim(
        buffer, jnp.where(is_live, new_value, old_value), slot_clip, 0
    )


def slope_of(pre_acts):
    pre_f = pre_acts.astype(jnp.float32)
    sigmoid_z = jax.nn.sigmoid(pre_f)
    return sigmoid_z * (1.0 + pre_f * (1.0 - sigmoid_z))


def on_device(layer_in, pre_act, weight, gain, cot_top):
    section_count = lax.axis_size("section")
    section_idx = lax.axis_index("section")
    dp_count = lax.axis_size("dp")
    inputs = layer_in[0]
    weight_rows = weight[0]
    gain_row = gain[0]
    micro_count, row_count, model_width = inputs.shape
    tick_count = section_count + micro_count - 1
    all_rows = row_count * dp_count
    inputs_f = inputs.astype(jnp.float32)
    row_scale = lax.rsqrt(jnp.mean(inputs_f * inputs_f, axis=-1, keepdims=True) + norm_eps)
    normed = (inputs_f * row_scale * gain_row).astype(jnp.bfloat16)
    top_full = lax.all_gather(cot_top, "section", axis=2, tiled=True)
    is_last = section_idx == section_count - 1
    is_first = section_idx == 0
    contract = (((1,), (1,)), ((), ()))
    slope_all = slope_of(pre_act[0])
    normed_cols = lax.all_to_all(normed, "dp", split_axis=2, concat_axis=1, tiled=True)

    def tick_step(tick_num, loop_state):
        received, grad_store, gain_acc, bottom_store = loop_state
        slot_pos = tick_num - (section_count - 1 - section_idx)
        is_live = (slot_pos >= 0) & (slot_pos < micro_count)
        slot_clip = jnp.clip(slot_pos, 0, micro_count - 1)
        incoming = jnp.where(is_last, pick_slot(top_full, slot_clip), received)
        pre_grad = (incoming.astype(jnp.float32) * pick_slot(slope_all, slot_clip)).astype(
            jnp.bfloat16
        )
        grad_all = lax.all_gather(pre_grad, "dp", axis=0, tiled=True)
        norm_cols = lax.dot_general(
            grad_all, weight_rows, contract, preferred_element_type=jnp.float32
        )
        norm_grad = lax.all_to_all(norm_cols, "dp", split_axis=0, concat_axis=1, tiled=True)
        scaled = gain_row * norm_grad
        inputs_here = pick_slot(inputs_f, slot_clip)
        scale_here = pick_slot(row_scale, slot_clip)
        row_dot = jnp.sum(scaled * inputs_here, axis=-1, keepdims=True)
        cubed = scale_here * scale_here * scale_here
        out_grad = (
            incoming.astype(jnp.float32)
            + scale_here * scaled
            - inputs_here * cubed * row_dot / model_width
        ).astype(jnp.bfloat16)
        gain_acc = gain_acc + jnp.where(
            is_live, jnp.sum(norm_grad * inputs_here * scale_here, axis=0), 0.0
        )
        grad_store = put_slot(grad_store, grad_all, slot_clip, is_live)
        bottom_store = put_slot(bottom_store, out_grad, slot_clip, is_live & is_first)
        return (pass_down(out_grad), grad_store, gain_acc, bottom_store)

    initial = (
        jnp.zeros((row_count, model_width), jnp.bfloat16),
        jnp.zeros((micro_count, all_rows, model_width), jnp.bfloat16),
        jnp.zeros((model_width,), jnp.float32),
        jnp.zeros((micro_count, row_count, model_width), jnp.bfloat16),
    )
    final_state = lax.fori_loop(0, tick_count, tick_step, initial)
    grad_store = final_state[1]
    gain_grad = lax.psum_scatter(final_state[2], "dp", scatter_dimension=0, tiled=True)
    bottom = final_state[3]
    weight_grad = jnp.einsum(
        "mki,mkj->ij", normed_cols, grad_store, preferred_element_type=jnp.float32
    ).astype(jnp.bfloat16)
    own_block = lax.psum_scatter(
        bottom.astype(jnp.float32).astype(jnp.bfloat16), "section", scatter_dimension=2, tiled=True
    )
    return (own_block, weight_grad[None], gain_grad[None])


def solution(mesh):
    return jax.shard_map(
        on_device,
        mesh=mesh,
        in_specs=(
            P("section", None, "dp", None),
            P("section", None, "dp", None),
            P("section", "dp", None),
            P("section", None),
            P(None, "dp", "section"),
        ),
        out_specs=(P(None, "dp", "section"), P("section", "dp", None), P("section", "dp")),
        check_vma=False,
    )
```

profile of v0, /device:TPU:64, one launch (start us, length us, event | category | flops | bytes accessed | tf_op | source)
XLA Modules:
  0.0 1945.2 jit_solution(1706129284291410059)
XLA Ops:
  7.9 11.9 copy.23
  19.8 10.0 multiply_reduce_fusion
  29.9 18.5 fusion.19
  48.5 14.9 reshape.90
  63.4 13.8 bitcast_convert_fusion.1
  77.2 14.9 copy.27
  101.1 1702.0 %while.22 = (s32[]{:T(128)}, bf16[8,6144]{1,0:T(8,128)(2,1)S(1)}, bf16[16,64,6144]{2,1,0:T(8,128)(2,1)}, f32[6144]{0:T(1024)S(1)}, bf16[16,8,6144]{2,1,0:T(8,128...) while((s32[]{:T(128)}, bf16[8,6144]{1,0:T(8,128)(2,1)S(1)}, ...), condition=%wide.region_4.5_spmd.clone, body=%wide.region_1.4_spmd.clone.sunk | while | flops 605417472 | bytes 19023856 | solution.py:93
  102.2 30.4 %all_gather.15 = bf16[64,6144]{1,0:T(8,128)(2,1)S(1)} all-gather(bf16[8,6144]{1,0:T(8,128)(2,1)S(1)} %fusion.30), channel_id=1, replica_groups=mesh['dp'=8,'section'=16] {'dp'}, dimensions={0}, use_global_device_ids=true | all-gather | bytes 884736 | tf_op jit(solution)/shard_map/while/body/eval_jaxpr/all_gather | solution.py:65
  158.9 29.8 %all_gather.15 = bf16[64,6144]{1,0:T(8,128)(2,1)S(1)} all-gather(bf16[8,6144]{1,0:T(8,128)(2,1)S(1)} %fusion.30), channel_id=1, replica_groups=mesh['dp'=8,'section'=16] {'dp'}, dimensions={0}, use_global_device_ids=true | all-gather | bytes 884736 | tf_op jit(solution)/shard_map/while/body/eval_jaxpr/all_gather | solution.py:65
  213.7 29.8 %all_gather.15 = bf16[64,6144]{1,0:T(8,128)(2,1)S(1)} all-gather(bf16[8,6144]{1,0:T(8,128)(2,1)S(1)} %fusion.30), channel_id=1, replica_groups=mesh['dp'=8,'section'=16] {'dp'}, dimensions={0}, use_global_device_ids=true | all-gather | bytes 884736 | tf_op jit(solution)/shard_map/while/body/eval_jaxpr/all_gather | solution.py:65
  268.5 29.9 %all_gather.15 = bf16[64,6144]{1,0:T(8,128)(2,1)S(1)} all-gather(bf16[8,6144]{1,0:T(8,128)(2,1)S(1)} %fusion.30), channel_id=1, replica_groups=mesh['dp'=8,'section'=16] {'dp'}, dimensions={0}, use_global_device_ids=true | all-gather | bytes 884736 | tf_op jit(solution)/shard_map/while/body/eval_jaxpr/all_gather | solution.py:65
  323.4 29.8 %all_gather.15 = bf16[64,6144]{1,0:T(8,128)(2,1)S(1)} all-gather(bf16[8,6144]{1,0:T(8,128)(2,1)S(1)} %fusion.30), channel_id=1, replica_groups=mesh['dp'=8,'section'=16] {'dp'}, dimensions={0}, use_global_device_ids=true | all-gather | bytes 884736 | tf_op jit(solution)/shard_map/while/body/eval_jaxpr/all_gather | solution.py:65
  378.2 29.8 %all_gather.15 = bf16[64,6144]{1,0:T(8,128)(2,1)S(1)} all-gather(bf16[8,6144]{1,0:T(8,128)(2,1)S(1)} %fusion.30), channel_id=1, replica_groups=mesh['dp'=8,'section'=16] {'dp'}, dimensions={0}, use_global_device_ids=true | all-gather | bytes 884736 | tf_op jit(solution)/shard_map/while/body/eval_jaxpr/all_gather | solution.py:65
  433.0 29.8 %all_gather.15 = bf16[64,6144]{1,0:T(8,128)(2,1)S(1)} all-gather(bf16[8,6144]{1,0:T(8,128)(2,1)S(1)} %fusion.30), channel_id=1, replica_groups=mesh['dp'=8,'section'=16] {'dp'}, dimensions={0}, use_global_device_ids=true | all-gather | bytes 884736 | tf_op jit(solution)/shard_map/while/body/eval_jaxpr/all_gather | solution.py:65
  487.9 30.0 %all_gather.15 = bf16[64,6144]{1,0:T(8,128)(2,1)S(1)} all-gather(bf16[8,6144]{1,0:T(8,128)(2,1)S(1)} %fusion.30), channel_id=1, replica_groups=mesh['dp'=8,'section'=16] {'dp'}, dimensions={0}, use_global_device_ids=true | all-gather | bytes 884736 | tf_op jit(solution)/shard_map/while/body/eval_jaxpr/all_gather | solution.py:65
  542.9 29.8 %all_gather.15 = bf16[64,6144]{1,0:T(8,128)(2,1)S(1)} all-gather(bf16[8,6144]{1,0:T(8,128)(2,1)S(1)} %fusion.30), channel_id=1, replica_groups=mesh['dp'=8,'section'=16] {'dp'}, dimensions={0}, use_global_device_ids=true | all-gather | bytes 884736 | tf_op jit(solution)/shard_map/while/body/eval_jaxpr/all_gather | solution.py:65
  597.7 30.0 %all_gather.15 = bf16[64,6144]{1,0:T(8,128)(2,1)S(1)} all-gather(bf16[8,6144]{1,0:T(8,128)(2,1)S(1)} %fusion.30), channel_id=1, replica_groups=mesh['dp'=8,'section'=16] {'dp'}, dimensions={0}, use_global_device_ids=true | all-gather | bytes 884736 | tf_op jit(solution)/shard_map/while/body/eval_jaxpr/all_gather | solution.py:65
  627.7 7.3 convolution_bitcast_fusion.2
  652.7 29.8 %all_gather.15 = bf16[64,6144]{1,0:T(8,128)(2,1)S(1)} all-gather(bf16[8,6144]{1,0:T(8,128)(2,1)S(1)} %fusion.30), channel_id=1, replica_groups=mesh['dp'=8,'section'=16] {'dp'}, dimensions={0}, use_global_device_ids=true | all-gather | bytes 884736 | tf_op jit(solution)/shard_map/while/body/eval_jaxpr/all_gather | solution.py:65
  707.5 29.9 %all_gather.15 = bf16[64,6144]{1,0:T(8,128)(2,1)S(1)} all-gather(bf16[8,6144]{1,0:T(8,128)(2,1)S(1)} %fusion.30), channel_id=1, replica_groups=mesh['dp'=8,'section'=16] {'dp'}, dimensions={0}, use_global_device_ids=true | all-gather | bytes 884736 | tf_op jit(solution)/shard_map/while/body/eval_jaxpr/all_gather | solution.py:65
  762.4 29.8 %all_gather.15 = bf16[64,6144]{1,0:T(8,128)(2,1)S(1)} all-gather(bf16[8,6144]{1,0:T(8,128)(2,1)S(1)} %fusion.30), channel_id=1, replica_groups=mesh['dp'=8,'section'=16] {'dp'}, dimensions={0}, use_global_device_ids=true | all-gather | bytes 884736 | tf_op jit(solution)/shard_map/while/body/eval_jaxpr/all_gather | solution.py:65
  817.2 29.7 %all_gather.15 = bf16[64,6144]{1,0:T(8,128)(2,1)S(1)} all-gather(bf16[8,6144]{1,0:T(8,128)(2,1)S(1)} %fusion.30), channel_id=1, replica_groups=mesh['dp'=8,'section'=16] {'dp'}, dimensions={0}, use_global_device_ids=true | all-gather | bytes 884736 | tf_op jit(solution)/shard_map/while/body/eval_jaxpr/all_gather | solution.py:65
  871.9 29.8 %all_gather.15 = bf16[64,6144]{1,0:T(8,128)(2,1)S(1)} all-gather(bf16[8,6144]{1,0:T(8,128)(2,1)S(1)} %fusion.30), channel_id=1, replica_groups=mesh['dp'=8,'section'=16] {'dp'}, dimensions={0}, use_global_device_ids=true | all-gather | bytes 884736 | tf_op jit(solution)/shard_map/while/body/eval_jaxpr/all_gather | solution.py:65
  926.7 29.7 %all_gather.15 = bf16[64,6144]{1,0:T(8,128)(2,1)S(1)} all-gather(bf16[8,6144]{1,0:T(8,128)(2,1)S(1)} %fusion.30), channel_id=1, replica_groups=mesh['dp'=8,'section'=16] {'dp'}, dimensions={0}, use_global_device_ids=true | all-gather | bytes 884736 | tf_op jit(solution)/shard_map/while/body/eval_jaxpr/all_gather | solution.py:65
  981.5 29.8 %all_gather.15 = bf16[64,6144]{1,0:T(8,128)(2,1)S(1)} all-gather(bf16[8,6144]{1,0:T(8,128)(2,1)S(1)} %fusion.30), channel_id=1, replica_groups=mesh['dp'=8,'section'=16] {'dp'}, dimensions={0}, use_global_device_ids=true | all-gather | bytes 884736 | tf_op jit(solution)/shard_map/while/body/eval_jaxpr/all_gather | solution.py:65
  1011.4 7.3 convolution_bitcast_fusion.2
  1036.4 29.8 %all_gather.15 = bf16[64,6144]{1,0:T(8,128)(2,1)S(1)} all-gather(bf16[8,6144]{1,0:T(8,128)(2,1)S(1)} %fusion.30), channel_id=1, replica_groups=mesh['dp'=8,'section'=16] {'dp'}, dimensions={0}, use_global_device_ids=true | all-gather | bytes 884736 | tf_op jit(solution)/shard_map/while/body/eval_jaxpr/all_gather | solution.py:65
  1066.2 7.3 convolution_bitcast_fusion.2
  1091.2 30.0 %all_gather.15 = bf16[64,6144]{1,0:T(8,128)(2,1)S(1)} all-gather(bf16[8,6144]{1,0:T(8,128)(2,1)S(1)} %fusion.30), channel_id=1, replica_groups=mesh['dp'=8,'section'=16] {'dp'}, dimensions={0}, use_global_device_ids=true | all-gather | bytes 884736 | tf_op jit(solution)/shard_map/while/body/eval_jaxpr/all_gather | solution.py:65
  1146.2 29.8 %all_gather.15 = bf16[64,6144]{1,0:T(8,128)(2,1)S(1)} all-gather(bf16[8,6144]{1,0:T(8,128)(2,1)S(1)} %fusion.30), channel_id=1, replica_groups=mesh['dp'=8,'section'=16] {'dp'}, dimensions={0}, use_global_device_ids=true | all-gather | bytes 884736 | tf_op jit(solution)/shard_map/while/body/eval_jaxpr/all_gather | solution.py:65
  1201.1 29.8 %all_gather.15 = bf16[64,6144]{1,0:T(8,128)(2,1)S(1)} all-gather(bf16[8,6144]{1,0:T(8,128)(2,1)S(1)} %fusion.30), channel_id=1, replica_groups=mesh['dp'=8,'section'=16] {'dp'}, dimensions={0}, use_global_device_ids=true | all-gather | bytes 884736 | tf_op jit(solution)/shard_map/while/body/eval_jaxpr/all_gather | solution.py:65
  1255.9 29.8 %all_gather.15 = bf16[64,6144]{1,0:T(8,128)(2,1)S(1)} all-gather(bf16[8,6144]{1,0:T(8,128)(2,1)S(1)} %fusion.30), channel_id=1, replica_groups=mesh['dp'=8,'section'=16] {'dp'}, dimensions={0}, use_global_device_ids=true | all-gather | bytes 884736 | tf_op jit(solution)/shard_map/while/body/eval_jaxpr/all_gather | solution.py:65
  1310.7 29.8 %all_gather.15 = bf16[64,6144]{1,0:T(8,128)(2,1)S(1)} all-gather(bf16[8,6144]{1,0:T(8,128)(2,1)S(1)} %fusion.30), channel_id=1, replica_groups=mesh['dp'=8,'section'=16] {'dp'}, dimensions={0}, use_global_device_ids=true | all-gather | bytes 884736 | tf_op jit(solution)/shard_map/while/body/eval_jaxpr/all_gather | solution.py:65
  1365.5 29.8 %all_gather.15 = bf16[64,6144]{1,0:T(8,128)(2,1)S(1)} all-gather(bf16[8,6144]{1,0:T(8,128)(2,1)S(1)} %fusion.30), channel_id=1, replica_groups=mesh['dp'=8,'section'=16] {'dp'}, dimensions={0}, use_global_device_ids=true | all-gather | bytes 884736 | tf_op jit(solution)/shard_map/while/body/eval_jaxpr/all_gather | solution.py:65
  1420.3 29.8 %all_gather.15 = bf16[64,6144]{1,0:T(8,128)(2,1)S(1)} all-gather(bf16[8,6144]{1,0:T(8,128)(2,1)S(1)} %fusion.30), channel_id=1, replica_groups=mesh['dp'=8,'section'=16] {'dp'}, dimensions={0}, use_global_device_ids=true | all-gather | bytes 884736 | tf_op jit(solution)/shard_map/while/body/eval_jaxpr/all_gather | solution.py:65
  1475.1 29.8 %all_gather.15 = bf16[64,6144]{1,0:T(8,128)(2,1)S(1)} all-gather(bf16[8,6144]{1,0:T(8,128)(2,1)S(1)} %fusion.30), channel_id=1, replica_groups=mesh['dp'=8,'section'=16] {'dp'}, dimensions={0}, use_global_device_ids=true | all-gather | bytes 884736 | tf_op jit(solution)/shard_map/while/body/eval_jaxpr/all_gather | solution.py:65
  1529.9 30.0 %all_gather.15 = bf16[64,6144]{1,0:T(8,128)(2,1)S(1)} all-gather(bf16[8,6144]{1,0:T(8,128)(2,1)S(1)} %fusion.30), channel_id=1, replica_groups=mesh['dp'=8,'section'=16] {'dp'}, dimensions={0}, use_global_device_ids=true | all-gather | bytes 884736 | tf_op jit(solution)/shard_map/while/body/eval_jaxpr/all_gather | solution.py:65
  1584.9 29.7 %all_gather.15 = bf16[64,6144]{1,0:T(8,128)(2,1)S(1)} all-gather(bf16[8,6144]{1,0:T(8,128)(2,1)S(1)} %fusion.30), channel_id=1, replica_groups=mesh['dp'=8,'section'=16] {'dp'}, dimensions={0}, use_global_device_ids=true | all-gather | bytes 884736 | tf_op jit(solution)/shard_map/while/body/eval_jaxpr/all_gather | solution.py:65
  1639.6 29.8 %all_gather.15 = bf16[64,6144]{1,0:T(8,128)(2,1)S(1)} all-gather(bf16[8,6144]{1,0:T(8,128)(2,1)S(1)} %fusion.30), channel_id=1, replica_groups=mesh['dp'=8,'section'=16] {'dp'}, dimensions={0}, use_global_device_ids=true | all-gather | bytes 884736 | tf_op jit(solution)/shard_map/while/body/eval_jaxpr/all_gather | solution.py:65
  1694.4 29.7 %all_gather.15 = bf16[64,6144]{1,0:T(8,128)(2,1)S(1)} all-gather(bf16[8,6144]{1,0:T(8,128)(2,1)S(1)} %fusion.30), channel_id=1, replica_groups=mesh['dp'=8,'section'=16] {'dp'}, dimensions={0}, use_global_device_ids=true | all-gather | bytes 884736 | tf_op jit(solution)/shard_map/while/body/eval_jaxpr/all_gather | solution.py:65
  1749.1 30.0 %all_gather.15 = bf16[64,6144]{1,0:T(8,128)(2,1)S(1)} all-gather(bf16[8,6144]{1,0:T(8,128)(2,1)S(1)} %fusion.30), channel_id=1, replica_groups=mesh['dp'=8,'section'=16] {'dp'}, dimensions={0}, use_global_device_ids=true | all-gather | bytes 884736 | tf_op jit(solution)/shard_map/while/body/eval_jaxpr/all_gather | solution.py:65
  1779.1 7.3 convolution_bitcast_fusion.2
  1806.9 19.6 %copy.29 = bf16[16,8,6144]{1,0,2:T(8,128)(2,1)} copy(bf16[16,8,6144]{2,1,0:T(8,128)(2,1)S(1)} %get-tuple-element.322) | data formatting | bytes 3145728
  1826.6 30.6 %reshape.87 = bf16[6144,128]{1,0:T(8,128)(2,1)} reshape(bf16[6144,16,8]{2,1,0:T(8,128)(2,1)} %bitcast.112) | data formatting | bytes 3145728
  1858.5 10.3 reshape.91
  1868.8 13.1 copy.28
  1882.0 34.5 %all-reduce = f32[6144]{0:T(1024)S(1)} all-reduce(f32[6144]{0:T(1024)S(1)} %get-tuple-element.324), channel_id=3, replica_groups=mesh['dp'=8,'section'=16] {'dp'}, use_global_device_ids=true, to_apply=%region_6.7.clone | all-reduce | flops 6144 | bytes 49152
  1917.1 16.8 fusion.9
  (520 shorter events, 764.6 us)
Async XLA Ops:
  7.2 87.6 %all-gather.2.cloned.1.call-start = ((), (), s32[]{:S(2)}) async-start(), calls=%async_computation.3 | async-start | bytes 1671168 | tf_op jit(solution)/shard_map/all_gather | solution.py:49
  139.9 11.6 all-to-all-start
  153.7 4.1 collective-permute-start
  196.0 10.3 all-to-all-start
  208.6 4.1 collective-permute-start
  250.9 10.3 all-to-all-start
  263.4 4.1 collective-permute-start
  305.7 10.3 all-to-all-start
  318.3 4.1 collective-permute-start
  360.5 10.3 all-to-all-start
  373.1 4.1 collective-permute-start
  415.3 10.3 all-to-all-start
  427.9 4.1 collective-permute-start
  470.2 10.3 all-to-all-start
  482.7 4.1 collective-permute-start
  525.2 10.3 all-to-all-start
  537.7 4.1 collective-permute-start
  580.0 10.3 all-to-all-start
  592.5 4.1 collective-permute-start
  635.0 10.3 all-to-all-start
  647.6 4.1 collective-permute-start
  689.8 10.3 all-to-all-start
  702.4 4.1 collective-permute-start
  744.7 10.3 all-to-all-start
  757.3 4.1 collective-permute-start
  799.5 10.3 all-to-all-start
  812.1 4.1 collective-permute-start
  854.2 10.3 all-to-all-start
  866.8 4.1 collective-permute-start
  909.1 10.3 all-to-all-start
  963.8 10.3 all-to-all-start
  1018.7 10.3 all-to-all-start
  1073.5 10.3 all-to-all-start
  1128.5 10.3 all-to-all-start
  1183.4 10.3 all-to-all-start
  1238.2 10.3 all-to-all-start
  1293.0 10.3 all-to-all-start
  1347.8 10.3 all-to-all-start
  1402.6 10.3 all-to-all-start
  1457.4 10.3 all-to-all-start
  1512.2 10.3 all-to-all-start
  1567.2 10.3 all-to-all-start
  1621.9 10.3 all-to-all-start
  1676.7 10.3 all-to-all-start
  1731.4 10.3 all-to-all-start
  1786.4 10.3 all-to-all-start
  1803.1 55.3 %all-to-all-start.1 = ((bf16[8,2,49152]{2,1,0:T(2,128)(2,1)}), bf16[8,2,49152]{2,1,0:T(2,128)(2,1)S(1)}, u32[]{:S(2)}, u32[]{:S(2)}) async-start(bf16[8,2,49152]{2,1,0:T(2,128)(2,1)} %reshape.90), calls=%async_computation.1 | async-start | bytes 3145728 | tf_op jit(solution)/shard_map/all_to_all | solution.py:54
  1806.7 127.2 %reduce-scatter.4.cloned.1.call-start = ((), (), s32[]{:S(2)}) async-start(), calls=%async_computation.4 | async-start | bytes 1671168
  (21 other events, 147.6 us)
Sparse Core Ops, SparseCore 0:
  10.3 46.4 all-gather.1
  1857.3 70.2 reduce-scatter.3
where the time goes:
time: 1960 us; the launch traced here: 1950 us
  blocking collectives  960 us (49%)
  matrix products  244 us (12%)
  waiting for transfers between devices  209 us (11%)
  other arithmetic  181 us (9%)
  starting transfers between devices  170 us (9%)
  local copies, waits for them, and re-layouts  165 us (8%)
    all_gather x31, blocking collectives, tick_step(): grad_all = lax.all_gather(pre_grad, 'dp', axis=0, tiled=True)  925 us
    dot_general x31, matrix products, tick_step(): lax.dot_general(grad_all, weight_rows, contract, preferred_element_type=j...  227 us
    all_to_all x31, waiting for transfers between devices, tick_step(): lax.all_to_all(norm_cols, 'dp', split_axis=0, concat_axis=1, tiled=True)  141 us
    unnamed x19, local copies, waits for them, and re-layouts  107 us
    all_to_all x31, starting transfers between devices, tick_step(): lax.all_to_all(norm_cols, 'dp', split_axis=0, concat_axis=1, tiled=True)  106 us
    ppermute x31, waiting for transfers between devices, shifted(): lax.ppermute(value, axis, [(source, source + steps) for source in range(l...  67.5 us
    dynamic_update_slice x62, other arithmetic, put_slot(): lax.dynamic_update_index_in_dim(buffer, jnp.where(is_live, new_value, old...  66 us
    ppermute x31, starting transfers between devices, shifted(): lax.ppermute(value, axis, [(source, source + steps) for source in range(l...  59.5 us
  transfers between devices with their start and end apart: 65, of which 62 were waited for; matrix products, arithmetic and copies ran while one was open for 13% of the time, Pallas kernels for 0%

commit v1 on v0

v1 whole, which is shorter than its diff:
```python
import jax
import jax.numpy as jnp
from jax import lax
from jax.experimental import pallas as pl
from jax.experimental.pallas import tpu as pltpu
from jax.sharding import PartitionSpec as P

norm_eps = 1e-05
LANES = 128
EXTRA = 16


def pass_down(value):
    count = lax.axis_size("section")
    return lax.ppermute(value, "section", [(source, source - 1) for source in range(1, count)])


def spread(value):
    count = lax.axis_size("dp")
    copies = jnp.broadcast_to(value[None], (count,) + value.shape)
    return lax.all_to_all(copies, "dp", split_axis=0, concat_axis=0, tiled=True)


def slope_of(pre_acts):
    pre_f = pre_acts.astype(jnp.float32)
    sigmoid_z = jax.nn.sigmoid(pre_f)
    return sigmoid_z * (1.0 + pre_f * (1.0 - sigmoid_z))


def split3(value):
    high = value.astype(jnp.bfloat16)
    rest = value - high.astype(jnp.float32)
    mid = rest.astype(jnp.bfloat16)
    low = (rest - mid.astype(jnp.float32)).astype(jnp.bfloat16)
    return jnp.stack([high, mid, low])


def tick_kernel(tokens, parts, width):
    cols = width // parts
    pieces = cols // LANES
    body_rows = pieces * tokens
    rows = body_rows + EXTRA
    across = (((1,), (1,)), ((), ()))
    down = (((0,), (0,)), ((), ()))

    def body(live, gathered, upper, weight_t, part, x_upper, x_own, scale, gain, acc_in, part_out, pre_out, acc_out):
        sums = jnp.concatenate([gathered[d, body_rows:rows, :] for d in range(parts)], axis=0)
        coef = lax.dot_general(
            sums, jnp.ones((parts * EXTRA, LANES), jnp.bfloat16), down, preferred_element_type=jnp.float32
        )[:tokens]
        for d in range(parts):
            for j in range(pieces):
                at = (d * pieces + j) * LANES
                piece = gathered[d, j * tokens : (j + 1) * tokens, :].astype(jnp.float32)
                piece = piece - coef * upper[:, at : at + LANES].astype(jnp.float32)
                pre_out[:, at : at + LANES] = piece.astype(jnp.bfloat16)
        norm_grad = jnp.dot(pre_out[...], weight_t[...], preferred_element_type=jnp.float32)
        scale_v = scale[...]
        total = jnp.zeros((tokens, LANES), jnp.float32)
        for j in range(pieces):
            here = slice(j * tokens, (j + 1) * tokens)
            lanes = slice(j * LANES, (j + 1) * LANES)
            grad_j = norm_grad[:, lanes]
            x_j = x_own[here, :].astype(jnp.float32)
            scaled = gain[:, lanes] * grad_j
            incoming = part[here, :].astype(jnp.float32) - coef * x_upper[here, :].astype(jnp.float32)
            part_out[here, :] = (incoming + scale_v * scaled).astype(jnp.bfloat16)
            total = total + scaled * x_j
            gain_sum = jnp.sum(grad_j * x_j * scale_v, axis=0, keepdims=True)
            acc_out[:, lanes] = acc_in[:, lanes] + jnp.where(live[0] > 0, gain_sum, 0.0)
        total = total * (scale_v * scale_v * scale_v * (1.0 / width))
        if tokens < LANES:
            total = jnp.concatenate([total, jnp.zeros((LANES - tokens, LANES), jnp.float32)], axis=0)
        high = total.astype(jnp.bfloat16)
        low = (total - high.astype(jnp.float32)).astype(jnp.bfloat16)
        ones = jnp.ones((EXTRA, LANES), jnp.bfloat16)
        line = lax.dot_general(ones, high, across, preferred_element_type=jnp.float32)
        line = line + lax.dot_general(ones, low, across, preferred_element_type=jnp.float32)
        line_high = line.astype(jnp.bfloat16).astype(jnp.float32)
        row = lax.broadcasted_iota(jnp.int32, (EXTRA, LANES), 0)
        packed = jnp.where(row == 0, line_high, jnp.where(row == 1, line - line_high, 0.0))
        part_out[body_rows:rows, :] = packed.astype(jnp.bfloat16)

    vmem = pl.BlockSpec(memory_space=pltpu.VMEM)
    return pl.pallas_call(
        body,
        out_shape=(
            jax.ShapeDtypeStruct((rows, LANES), jnp.bfloat16),
            jax.ShapeDtypeStruct((tokens, width), jnp.bfloat16),
            jax.ShapeDtypeStruct((1, cols), jnp.float32),
        ),
        in_specs=[pl.BlockSpec(memory_space=pltpu.SMEM)] + [vmem] * 9,
        out_specs=(vmem, vmem, vmem),
        name="tick",
        cost_estimate=pl.CostEstimate(flops=2 * tokens * width * cols, bytes_accessed=4 * width * tokens, transcendentals=0),
        compiler_params=pltpu.CompilerParams(vmem_limit_bytes=32 * 1024 * 1024),
    )


def on_device(layer_in, pre_act, weight, gain, cot_top):
    sections = lax.axis_size("section")
    parts = lax.axis_size("dp")
    section_idx = lax.axis_index("section")
    dp_idx = lax.axis_index("dp")
    inputs = layer_in[0]
    pre_acts = pre_act[0]
    micro, own_rows, width = inputs.shape
    tokens = own_rows * parts
    cols = width // parts
    pieces = cols // LANES
    share = sections // parts
    share_pieces = pieces // share
    body_rows = pieces * tokens
    local = micro * own_rows
    is_last = section_idx == sections - 1
    gain_cols = lax.dynamic_slice_in_dim(gain, dp_idx * cols, cols, axis=1)
    weight_t = weight[0].T

    inputs_f = inputs.astype(jnp.float32)
    mean_sq = jnp.mean(inputs_f * inputs_f, axis=-1).reshape(1, local)
    side = split3(mean_sq)[:, 0]
    side = jnp.pad(side, ((0, 13), (0, cols - local)))

    def by_target(value):
        return value.reshape(local, parts, cols).transpose(1, 0, 2)

    message = jnp.concatenate(
        [by_target(pre_acts), by_target(inputs), jnp.broadcast_to(side[None], (parts,) + side.shape)], axis=1
    )
    got = lax.all_to_all(message, "dp", split_axis=0, concat_axis=0, tiled=True)

    def as_pieces(value, count):
        value = value.reshape(parts, micro, own_rows, count, LANES)
        return value.transpose(1, 3, 0, 2, 4).reshape(micro, count * tokens, LANES)

    slope = slope_of(as_pieces(got[:, :local], pieces))
    slope = jnp.pad(slope, ((0, 0), (0, EXTRA), (0, 0)), constant_values=1.0)
    x_pieces = as_pieces(got[:, local : 2 * local], pieces)
    x_cols = got[:, local : 2 * local].reshape(parts, micro, own_rows, cols).transpose(1, 0, 2, 3)
    x_cols = x_cols.reshape(micro, tokens, cols)
    sq = jnp.sum(got[:, 2 * local : 2 * local + 3, :local].astype(jnp.float32), axis=1)
    sq = sq.reshape(parts, micro, own_rows).transpose(1, 0, 2).reshape(micro, tokens)
    row_scale = lax.rsqrt(sq + norm_eps)[..., None]
    scale_lanes = jnp.broadcast_to(row_scale, (micro, tokens, LANES))
    normed_cols = (x_cols.astype(jnp.float32) * row_scale * gain_cols).astype(jnp.bfloat16)

    x_upper = pass_down(x_pieces)
    inputs_upper = pass_down(inputs)
    upper_rows = (inputs_upper.astype(jnp.float32) * slope_of(pre_acts)).astype(jnp.bfloat16)
    upper_all = lax.all_gather(upper_rows, "dp", axis=0)

    top_all = as_pieces(spread(cot_top), share_pieces)
    top = []
    for i in range(share):
        pairs = [
            (d * sections + d * share + i, d * sections + sections - 1) for d in range(parts)
        ]
        top.append(lax.ppermute(top_all, ("dp", "section"), pairs))
    top = jnp.pad(jnp.concatenate(top, axis=1), ((0, 0), (0, EXTRA), (0, 0)))

    tick = tick_kernel(tokens, parts, width)

    def tick_step(tick_num, state):
        received, grad_store, gain_acc, bottom_store = state
        slot_pos = tick_num - (sections - 1 - section_idx)
        is_live = (slot_pos >= 0) & (slot_pos < micro)
        slot = jnp.clip(slot_pos, 0, micro - 1)
        pick = lambda buffer: lax.dynamic_index_in_dim(buffer, slot, 0, keepdims=False)
        part = jnp.where(is_last, pick(top), received)
        sent = (part.astype(jnp.float32) * pick(slope)).astype(jnp.bfloat16)
        gathered = spread(sent)
        upper = lax.dynamic_index_in_dim(upper_all, slot, 1, keepdims=False).reshape(tokens, width)
        part_new, pre_grad, gain_acc = tick(
            is_live.astype(jnp.int32).reshape(1),
            gathered,
            pltpu.with_memory_space_constraint(upper, pltpu.VMEM),
            pltpu.with_memory_space_constraint(weight_t, pltpu.VMEM),
            part,
            pick(x_upper),
            pick(x_pieces),
            pick(scale_lanes),
            gain_cols,
            gain_acc,
        )
        keep = jnp.where(slot_pos < micro, slot, micro)
        grad_store = lax.dynamic_update_index_in_dim(grad_store, pre_grad, keep, 0)
        bottom_store = lax.dynamic_update_index_in_dim(bottom_store, part_new, slot, 0)
        return (pass_down(part_new), grad_store, gain_acc, bottom_store)

    initial = (
        jnp.zeros((body_rows + EXTRA, LANES), jnp.bfloat16),
        jnp.zeros((micro + 1, tokens, width), jnp.bfloat16),
        jnp.zeros((1, cols), jnp.float32),
        jnp.zeros((micro, body_rows + EXTRA, LANES), jnp.bfloat16),
    )
    _, grad_store, gain_acc, bottom_store = lax.fori_loop(0, sections + micro - 1, tick_step, initial)

    own = jnp.sum(bottom_store[:, body_rows : body_rows + 2, :tokens].astype(jnp.float32), axis=1)
    own = jnp.sum(spread(own), axis=0)
    coef = jnp.tile(own, (1, pieces))[..., None]
    bottom = bottom_store[:, :body_rows].astype(jnp.float32) - coef * x_pieces.astype(jnp.float32)
    bottom = bottom.astype(jnp.bfloat16)
    part_rows = share_pieces * tokens
    mine = None
    for i in range(share):
        pairs = [(d * sections, d * sections + d * share + i) for d in range(parts)]
        moved = lax.ppermute(bottom[:, i * part_rows : (i + 1) * part_rows], ("dp", "section"), pairs)
        mine = moved if mine is None else jnp.where(section_idx % share == i, moved, mine)
    mine = mine.reshape(micro, share_pieces, parts, own_rows, LANES).transpose(2, 0, 3, 1, 4)
    mine = mine.reshape(parts, micro, own_rows, share_pieces * LANES)
    shares = lax.all_to_all(mine, "dp", split_axis=0, concat_axis=0, tiled=True)
    own_block = lax.dynamic_index_in_dim(shares, section_idx // share, 0, keepdims=False)

    weight_grad = jnp.einsum(
        "mki,mkj->ij", normed_cols, grad_store[:micro], preferred_element_type=jnp.float32
    ).astype(jnp.bfloat16)
    return (own_block, weight_grad[None], gain_acc)


def solution(mesh):
    return jax.shard_map(
        on_device,
        mesh=mesh,
        in_specs=(
            P("section", None, "dp", None),
            P("section", None, "dp", None),
            P("section", "dp", None),
            P("section", None),
            P(None, "dp", "section"),
        ),
        out_specs=(P(None, "dp", "section"), P("section", "dp", None), P("section", "dp")),
        check_vma=False,
    )
```

time: 1960 us -> 1280 us (0.65)
  blocking collectives: 960 us -> 9.38 us
  starting transfers between devices: 170 us -> 442 us
  matrix products: 244 us -> 17 us
  waiting for transfers between devices: 209 us -> 358 us
  local copies, waits for them, and re-layouts: 165 us -> 300 us
  other arithmetic: 181 us -> 51.5 us
  Pallas kernels: 0 us -> 67.8 us
    all_gather x31 -> x0, blocking collectives: 925 us -> none  [tick_step(): grad_all = lax.all_gather(pre_grad, 'dp', axis=0, tiled=True)]
    ppermute x31 -> x37, starting transfers between devices: 59.5 us -> 301 us  [the longest x33 295 us: pass_down(): lax.ppermute(value, 'section', [(source, source - 1) for source in range(...]
    dot_general x32 -> x1, matrix products: 244 us -> 17 us  [on_device(): jnp.einsum('mki,mkj->ij', normed_cols, grad_store[:micro], preferred_elem...]
    all_to_all x32 -> x34, waiting for transfers between devices: 141 us -> 320 us  [the longest x32 258 us: spread(): return lax.all_to_all(copies, 'dp', split_axis=0, concat_axis=0, tiled=True)]
    while x0 -> x93, local copies, waits for them, and re-layouts: none -> 114 us
    unnamed x19 -> x18, local copies, waits for them, and re-layouts: 107 us -> 13.5 us
    pallas_call x0 -> x31, Pallas kernels: none -> 67.8 us  [tick_step(): tick(is_live.astype(jnp.int32).reshape(1), gathered, pltpu.with_memory_sp...]
    dynamic_update_slice x62 -> x0, other arithmetic: 66 us -> none  [put_slot(): lax.dynamic_update_index_in_dim(buffer, jnp.where(is_live, new_value, old...]
  transfers between devices with their start and end apart: 65 -> 72, of which waited for: 62 -> 66; matrix products, arithmetic and copies ran while one was open for 13% -> 13% of each run, Pallas kernels for 0% -> 0%
where the time goes in v1:
time: 1280 us; the launch traced here: 1260 us
  starting transfers between devices  442 us (35%)
  waiting for transfers between devices  358 us (28%)
  local copies, waits for them, and re-layouts  300 us (23%)
  Pallas kernels  67.8 us (5%)
  other arithmetic  51.5 us (4%)
  matrix products  17 us (1%)
  between operations  14.3 us (1%)
    ppermute x33, starting transfers between devices, pass_down(): lax.ppermute(value, 'section', [(source, source - 1) for source in range(...  295 us
    all_to_all x32, waiting for transfers between devices, spread(): return lax.all_to_all(copies, 'dp', split_axis=0, concat_axis=0, tiled=True)  258 us
    all_to_all x32, starting transfers between devices, spread(): return lax.all_to_all(copies, 'dp', split_axis=0, concat_axis=0, tiled=True)  120 us
    while x93, local copies, waits for them, and re-layouts  114 us
    pallas_call x31, Pallas kernels, tick_step(): tick(is_live.astype(jnp.int32).reshape(1), gathered, pltpu.with_memory_sp...  67.8 us
    all_to_all x1, waiting for transfers between devices, on_device(): got = lax.all_to_all(message, 'dp', split_axis=0, concat_axis=0, tiled=True)  62 us
    ppermute x33, waiting for transfers between devices, pass_down(): lax.ppermute(value, 'section', [(source, source - 1) for source in range(...  38.5 us
    reshape x31, local copies, waits for them, and re-layouts, tick_step(): lax.dynamic_index_in_dim(upper_all, slot, 1, keepdims=False)  36.9 us
  transfers between devices with their start and end apart: 72, of which 66 were waited for; matrix products, arithmetic and copies ran while one was open for 13% of the time, Pallas kernels for 0%

profile of v1, /device:TPU:64, one launch (start us, length us, event | category | flops | bytes accessed | tf_op | source)
XLA Modules:
  0.0 1263.0 jit_solution(5539392981785746578)
XLA Ops:
  10.6 18.4 %collective-permute-done.3 = bf16[16,8,6144]{2,1,0:T(8,128)(2,1)S(1)} collective-permute-done((bf16[16,8,6144]{2,1,0:T(8,128)(2,1)}, bf16[16,8,6144]{2,1,0:T(8,128)(2,1)S(1)}, u32[]{:S(2)}, u32[]{:S(2)}) %collective-permute-start.3) | collective-permute-done | bytes 1572896 | tf_op jit(solution)/shard_map/ppermute | solution.py:15
  34.2 9.5 all-to-all-start.1
  47.5 9.7 all-to-all-done.1
  67.1 62.0 %all-to-all-done.2 = bf16[8,272,768]{2,1,0:T(8,128)(2,1)S(1)} async-done(((bf16[8,272,768]{2,1,0:T(8,128)(2,1)}), bf16[8,272,768]{2,1,0:T(8,128)(2,1)S(1)}, u32[]{:S(2)}, u32[]{:S(2)}) %all-to-all-start.2) | async-done | bytes 3342368 | tf_op jit(solution)/shard_map/all_to_all | solution.py:130
  134.2 99.3 %collective-permute-start.4 = (bf16[16,384,128]{2,1,0:T(8,128)(2,1)}, bf16[16,384,128]{2,1,0:T(8,128)(2,1)}, u32[]{:S(2)}, u32[]{:S(2)}) collective-permute-start(bf16[16,384,128]{2,1,0:T(8,128)(2,1)} %bitcast.23), channel_id=1, source_target_pairs={{1,0},{2,1},{3,2},{4,3},{5,4},{6,5},{7,6},{8,7},{9,8},{10,9},{11,1... | collective-permute-start | bytes 4718600 | tf_op jit(solution)/shard_map/ppermute | solution.py:15
  233.5 12.6 copy.58
  258.4 6.5 broadcast_in_dim.79
  266.3 934.1 %while.21 = (s32[]{:T(128)}, bf16[400,128]{1,0:T(8,128)(2,1)S(1)}, bf16[17,64,6144]{2,1,0:T(8,128)(2,1)}, f32[1,768]{1,0:T(1,128)S(1)}, bf16[16,400,128]{2,1,0:T...) while((s32[]{:T(128)}, bf16[400,128]{1,0:T(8,128)(2,1)S(1)}, ...), condition=%wide.region_3.4_spmd, body=%wide.region_2.3_spmd.sunk | while | flops 604184576 | bytes 47540596 | solution.py:196
  274.8 8.1 all-to-all-done.gathered
  304.5 8.0 all-to-all-done.gathered
  318.4 6.2 collective-permute-start
  334.6 8.0 all-to-all-done.gathered
  348.5 6.2 collective-permute-start
  364.7 8.0 all-to-all-done.gathered
  378.6 6.2 collective-permute-start
  394.8 8.0 all-to-all-done.gathered
  408.7 6.2 collective-permute-start
  425.0 8.0 all-to-all-done.gathered
  438.8 6.2 collective-permute-start
  455.1 8.0 all-to-all-done.gathered
  469.0 6.2 collective-permute-start
  485.2 8.0 all-to-all-done.gathered
  515.3 8.0 all-to-all-done.gathered
  545.5 8.0 all-to-all-done.gathered
  575.6 8.0 all-to-all-done.gathered
  605.7 8.0 all-to-all-done.gathered
  635.8 8.0 all-to-all-done.gathered
  665.9 8.0 all-to-all-done.gathered
  696.1 8.0 all-to-all-done.gathered
  726.2 8.0 all-to-all-done.gathered
  756.3 8.0 all-to-all-done.gathered
  786.4 8.0 all-to-all-done.gathered
  816.6 8.0 all-to-all-done.gathered
  846.7 8.0 all-to-all-done.gathered
  876.8 8.0 all-to-all-done.gathered
  906.9 8.0 all-to-all-done.gathered
  937.0 8.0 all-to-all-done.gathered
  967.2 8.0 all-to-all-done.gathered
  997.3 8.0 all-to-all-done.gathered
  1027.4 8.0 all-to-all-done.gathered
  1057.5 8.0 all-to-all-done.gathered
  1087.7 8.0 all-to-all-done.gathered
  1117.8 8.0 all-to-all-done.gathered
  1147.9 8.0 all-to-all-done.gathered
  1178.0 8.0 all-to-all-done.gathered
  1201.3 9.4 all_to_all.26
  1221.2 16.3 %all-to-all-start.4 = ((bf16[8,16,8,384]{3,2,1,0:T(8,128)(2,1)}), bf16[8,16,8,384]{3,2,1,0:T(8,128)(2,1)}, u32[]{:S(2)}, u32[]{:S(2)}) async-start(bf16[8,16,8,384]{3,2,1,0:T(8,128)(2,1)} %bitcast.104), calls=%async_computation.4 | async-start | bytes 1572864 | tf_op jit(solution)/shard_map/all_to_all | solution.py:211
  1237.5 17.0 %fusion.5 = bf16[1,768,6144]{2,1,0:T(8,128)(2,1)} fusion(bf16[17,64,6144]{2,1,0:T(8,128)(2,1)} %get-tuple-element.344, f32[16,8,8,768]{3,2,0,1:T(8,128)S(1)} %copy-done.4, f32[768]{0:T(1024)S(1)} %get-tuple-element.453, f32[16,64]{1,0:T(8,128)S(1)} %copy.57), kind=kOutput, calls=%fused_computation.12 | convolution fusion | flops 9670754304 | bytes 25172992 | tf_op jit(solution)/shard_map/mki,mkj->ij/dot_general | solution.py:214
  (500 shorter events, 700.7 us)
Async XLA Ops:
  7.2 251.0 %all-gather.3.cloned.1.call-start = ((), (), s32[]{:S(2)}) async-start(), calls=%async_computation.5 | async-start | bytes 14155776 | tf_op jit(solution)/shard_map/all_gather | solution.py:150
  7.2 21.7 %collective-permute-start.3 = (bf16[16,8,6144]{2,1,0:T(8,128)(2,1)}, bf16[16,8,6144]{2,1,0:T(8,128)(2,1)S(1)}, u32[]{:S(2)}, u32[]{:S(2)}) collective-permute-start(bf16[16,8,6144]{2,1,0:T(8,128)(2,1)} %bitcast.121), channel_id=1, source_target_pairs={{1,0},{2,1},{3,2},{4,3},{5,4},{6,5},{7,6},{8,7},{9,8},{10,9},{11,1... | collective-permute-start | bytes 4718600 | tf_op jit(solution)/shard_map/ppermute | solution.py:15
  34.2 23.0 %all-to-all-start.1 = ((bf16[8,16,8,384]{3,2,1,0:T(8,128)(2,1)}), bf16[8,16,8,384]{3,2,1,0:T(8,128)(2,1)}, u32[]{:S(2)}, u32[]{:S(2)}) async-start(bf16[8,16,8,384]{3,2,1,0:T(8,128)(2,1)} %broadcast_in_dim.82), calls=%async_computation.1 | async-start | bytes 1572864 | tf_op jit(solution)/shard_map/all_to_all | solution.py:21
  57.2 71.9 %all-to-all-start.2 = ((bf16[8,272,768]{2,1,0:T(8,128)(2,1)}), bf16[8,272,768]{2,1,0:T(8,128)(2,1)S(1)}, u32[]{:S(2)}, u32[]{:S(2)}) async-start(bf16[8,272,768]{2,1,0:T(8,128)(2,1)} %copy.53), calls=%async_computation.2 | async-start | bytes 6684672 | tf_op jit(solution)/shard_map/all_to_all | solution.py:130
  63.9 183.0 %collective-permute-start.2 = (bf16[16,192,128]{2,1,0:T(8,128)(2,1)}, bf16[16,192,128]{2,1,0:T(8,128)(2,1)}, u32[]{:S(2)}, u32[]{:S(2)}) collective-permute-start(bf16[16,192,128]{2,1,0:T(8,128)(2,1)} %bitcast.11), channel_id=1, source_target_pairs={{1,15},{19,31},{37,47},{55,63},{73,79},{91,95},{109,111},{127,127}} | collective-permute-start | bytes 2359304 | tf_op jit(solution)/shard_map/ppermute | solution.py:158
  65.5 181.5 %collective-permute-start.1 = (bf16[16,192,128]{2,1,0:T(8,128)(2,1)}, bf16[16,192,128]{2,1,0:T(8,128)(2,1)}, u32[]{:S(2)}, u32[]{:S(2)}) collective-permute-start(bf16[16,192,128]{2,1,0:T(8,128)(2,1)} %bitcast.11), channel_id=1, source_target_pairs={{0,15},{18,31},{36,47},{54,63},{72,79},{90,95},{108,111},{126,127}} | collective-permute-start | bytes 2359304 | tf_op jit(solution)/shard_map/ppermute | solution.py:158
  134.2 124.0 %collective-permute-start.4 = (bf16[16,384,128]{2,1,0:T(8,128)(2,1)}, bf16[16,384,128]{2,1,0:T(8,128)(2,1)}, u32[]{:S(2)}, u32[]{:S(2)}) collective-permute-start(bf16[16,384,128]{2,1,0:T(8,128)(2,1)} %bitcast.23), channel_id=1, source_target_pairs={{1,0},{2,1},{3,2},{4,3},{5,4},{6,5},{7,6},{8,7},{9,8},{10,9},{11,1... | collective-permute-start | bytes 4718600 | tf_op jit(solution)/shard_map/ppermute | solution.py:15
  268.3 14.6 %all-to-all-start = ((bf16[8,400,128]{2,1,0:T(8,128)(2,1)}), bf16[8,400,128]{2,1,0:T(8,128)(2,1)S(1)}, u32[]{:S(2)}, u32[]{:S(2)}) async-start(bf16[8,400,128]{2,1,0:T(8,128)(2,1)} %broadcast_in_dim.89), calls=%async_computation | async-start | bytes 1638400 | tf_op jit(solution)/shard_map/while/body/eval_jaxpr/all_to_all | solution.py:21
  298.7 13.8 %all-to-all-start = ((bf16[8,400,128]{2,1,0:T(8,128)(2,1)}), bf16[8,400,128]{2,1,0:T(8,128)(2,1)S(1)}, u32[]{:S(2)}, u32[]{:S(2)}) async-start(bf16[8,400,128]{2,1,0:T(8,128)(2,1)} %broadcast_in_dim.89), calls=%async_computation | async-start | bytes 1638400 | tf_op jit(solution)/shard_map/while/body/eval_jaxpr/all_to_all | solution.py:21
  328.8 13.8 %all-to-all-start = ((bf16[8,400,128]{2,1,0:T(8,128)(2,1)}), bf16[8,400,128]{2,1,0:T(8,128)(2,1)S(1)}, u32[]{:S(2)}, u32[]{:S(2)}) async-start(bf16[8,400,128]{2,1,0:T(8,128)(2,1)} %broadcast_in_dim.89), calls=%async_computation | async-start | bytes 1638400 | tf_op jit(solution)/shard_map/while/body/eval_jaxpr/all_to_all | solution.py:21
  348.5 8.5 collective-permute-start
  359.0 13.8 %all-to-all-start = ((bf16[8,400,128]{2,1,0:T(8,128)(2,1)}), bf16[8,400,128]{2,1,0:T(8,128)(2,1)S(1)}, u32[]{:S(2)}, u32[]{:S(2)}) async-start(bf16[8,400,128]{2,1,0:T(8,128)(2,1)} %broadcast_in_dim.89), calls=%async_computation | async-start | bytes 1638400 | tf_op jit(solution)/shard_map/while/body/eval_jaxpr/all_to_all | solution.py:21
  378.6 8.5 collective-permute-start
  389.1 13.8 %all-to-all-start = ((bf16[8,400,128]{2,1,0:T(8,128)(2,1)}), bf16[8,400,128]{2,1,0:T(8,128)(2,1)S(1)}, u32[]{:S(2)}, u32[]{:S(2)}) async-start(bf16[8,400,128]{2,1,0:T(8,128)(2,1)} %broadcast_in_dim.89), calls=%async_computation | async-start | bytes 1638400 | tf_op jit(solution)/shard_map/while/body/eval_jaxpr/all_to_all | solution.py:21
  408.7 8.5 collective-permute-start
  419.2 13.8 %all-to-all-start = ((bf16[8,400,128]{2,1,0:T(8,128)(2,1)}), bf16[8,400,128]{2,1,0:T(8,128)(2,1)S(1)}, u32[]{:S(2)}, u32[]{:S(2)}) async-start(bf16[8,400,128]{2,1,0:T(8,128)(2,1)} %broadcast_in_dim.89), calls=%async_computation | async-start | bytes 1638400 | tf_op jit(solution)/shard_map/while/body/eval_jaxpr/all_to_all | solution.py:21
  449.3 13.8 %all-to-all-start = ((bf16[8,400,128]{2,1,0:T(8,128)(2,1)}), bf16[8,400,128]{2,1,0:T(8,128)(2,1)S(1)}, u32[]{:S(2)}, u32[]{:S(2)}) async-start(bf16[8,400,128]{2,1,0:T(8,128)(2,1)} %broadcast_in_dim.89), calls=%async_computation | async-start | bytes 1638400 | tf_op jit(solution)/shard_map/while/body/eval_jaxpr/all_to_all | solution.py:21
  469.0 8.5 collective-permute-start
  479.5 13.8 %all-to-all-start = ((bf16[8,400,128]{2,1,0:T(8,128)(2,1)}), bf16[8,400,128]{2,1,0:T(8,128)(2,1)S(1)}, u32[]{:S(2)}, u32[]{:S(2)}) async-start(bf16[8,400,128]{2,1,0:T(8,128)(2,1)} %broadcast_in_dim.89), calls=%async_computation | async-start | bytes 1638400 | tf_op jit(solution)/shard_map/while/body/eval_jaxpr/all_to_all | solution.py:21
  499.1 8.5 collective-permute-start
  509.6 13.8 %all-to-all-start = ((bf16[8,400,128]{2,1,0:T(8,128)(2,1)}), bf16[8,400,128]{2,1,0:T(8,128)(2,1)S(1)}, u32[]{:S(2)}, u32[]{:S(2)}) async-start(bf16[8,400,128]{2,1,0:T(8,128)(2,1)} %broadcast_in_dim.89), calls=%async_computation | async-start | bytes 1638400 | tf_op jit(solution)/shard_map/while/body/eval_jaxpr/all_to_all | solution.py:21
  529.2 8.5 collective-permute-start
  539.7 13.8 %all-to-all-start = ((bf16[8,400,128]{2,1,0:T(8,128)(2,1)}), bf16[8,400,128]{2,1,0:T(8,128)(2,1)S(1)}, u32[]{:S(2)}, u32[]{:S(2)}) async-start(bf16[8,400,128]{2,1,0:T(8,128)(2,1)} %broadcast_in_dim.89), calls=%async_computation | async-start | bytes 1638400 | tf_op jit(solution)/shard_map/while/body/eval_jaxpr/all_to_all | solution.py:21
  569.8 13.8 %all-to-all-start = ((bf16[8,400,128]{2,1,0:T(8,128)(2,1)}), bf16[8,400,128]{2,1,0:T(8,128)(2,1)S(1)}, u32[]{:S(2)}, u32[]{:S(2)}) async-start(bf16[8,400,128]{2,1,0:T(8,128)(2,1)} %broadcast_in_dim.89), calls=%async_computation | async-start | bytes 1638400 | tf_op jit(solution)/shard_map/while/body/eval_jaxpr/all_to_all | solution.py:21
  589.4 8.5 collective-permute-start
  599.9 13.8 %all-to-all-start = ((bf16[8,400,128]{2,1,0:T(8,128)(2,1)}), bf16[8,400,128]{2,1,0:T(8,128)(2,1)S(1)}, u32[]{:S(2)}, u32[]{:S(2)}) async-start(bf16[8,400,128]{2,1,0:T(8,128)(2,1)} %broadcast_in_dim.89), calls=%async_computation | async-start | bytes 1638400 | tf_op jit(solution)/shard_map/while/body/eval_jaxpr/all_to_all | solution.py:21
  619.6 8.5 collective-permute-start
  630.1 13.8 %all-to-all-start = ((bf16[8,400,128]{2,1,0:T(8,128)(2,1)}), bf16[8,400,128]{2,1,0:T(8,128)(2,1)S(1)}, u32[]{:S(2)}, u32[]{:S(2)}) async-start(bf16[8,400,128]{2,1,0:T(8,128)(2,1)} %broadcast_in_dim.89), calls=%async_computation | async-start | bytes 1638400 | tf_op jit(solution)/shard_map/while/body/eval_jaxpr/all_to_all | solution.py:21
  649.7 8.5 collective-permute-start
  660.2 13.8 %all-to-all-start = ((bf16[8,400,128]{2,1,0:T(8,128)(2,1)}), bf16[8,400,128]{2,1,0:T(8,128)(2,1)S(1)}, u32[]{:S(2)}, u32[]{:S(2)}) async-start(bf16[8,400,128]{2,1,0:T(8,128)(2,1)} %broadcast_in_dim.89), calls=%async_computation | async-start | bytes 1638400 | tf_op jit(solution)/shard_map/while/body/eval_jaxpr/all_to_all | solution.py:21
  690.3 13.8 %all-to-all-start = ((bf16[8,400,128]{2,1,0:T(8,128)(2,1)}), bf16[8,400,128]{2,1,0:T(8,128)(2,1)S(1)}, u32[]{:S(2)}, u32[]{:S(2)}) async-start(bf16[8,400,128]{2,1,0:T(8,128)(2,1)} %broadcast_in_dim.89), calls=%async_computation | async-start | bytes 1638400 | tf_op jit(solution)/shard_map/while/body/eval_jaxpr/all_to_all | solution.py:21
  720.4 13.8 %all-to-all-start = ((bf16[8,400,128]{2,1,0:T(8,128)(2,1)}), bf16[8,400,128]{2,1,0:T(8,128)(2,1)S(1)}, u32[]{:S(2)}, u32[]{:S(2)}) async-start(bf16[8,400,128]{2,1,0:T(8,128)(2,1)} %broadcast_in_dim.89), calls=%async_computation | async-start | bytes 1638400 | tf_op jit(solution)/shard_map/while/body/eval_jaxpr/all_to_all | solution.py:21
  750.6 13.8 %all-to-all-start = ((bf16[8,400,128]{2,1,0:T(8,128)(2,1)}), bf16[8,400,128]{2,1,0:T(8,128)(2,1)S(1)}, u32[]{:S(2)}, u32[]{:S(2)}) async-start(bf16[8,400,128]{2,1,0:T(8,128)(2,1)} %broadcast_in_dim.89), calls=%async_computation | async-start | bytes 1638400 | tf_op jit(solution)/shard_map/while/body/eval_jaxpr/all_to_all | solution.py:21
  780.7 13.8 %all-to-all-start = ((bf16[8,400,128]{2,1,0:T(8,128)(2,1)}), bf16[8,400,128]{2,1,0:T(8,128)(2,1)S(1)}, u32[]{:S(2)}, u32[]{:S(2)}) async-start(bf16[8,400,128]{2,1,0:T(8,128)(2,1)} %broadcast_in_dim.89), calls=%async_computation | async-start | bytes 1638400 | tf_op jit(solution)/shard_map/while/body/eval_jaxpr/all_to_all | solution.py:21
  810.8 13.8 %all-to-all-start = ((bf16[8,400,128]{2,1,0:T(8,128)(2,1)}), bf16[8,400,128]{2,1,0:T(8,128)(2,1)S(1)}, u32[]{:S(2)}, u32[]{:S(2)}) async-start(bf16[8,400,128]{2,1,0:T(8,128)(2,1)} %broadcast_in_dim.89), calls=%async_computation | async-start | bytes 1638400 | tf_op jit(solution)/shard_map/while/body/eval_jaxpr/all_to_all | solution.py:21
  840.9 13.8 %all-to-all-start = ((bf16[8,400,128]{2,1,0:T(8,128)(2,1)}), bf16[8,400,128]{2,1,0:T(8,128)(2,1)S(1)}, u32[]{:S(2)}, u32[]{:S(2)}) async-start(bf16[8,400,128]{2,1,0:T(8,128)(2,1)} %broadcast_in_dim.89), calls=%async_computation | async-start | bytes 1638400 | tf_op jit(solution)/shard_map/while/body/eval_jaxpr/all_to_all | solution.py:21
  871.0 13.8 %all-to-all-start = ((bf16[8,400,128]{2,1,0:T(8,128)(2,1)}), bf16[8,400,128]{2,1,0:T(8,128)(2,1)S(1)}, u32[]{:S(2)}, u32[]{:S(2)}) async-start(bf16[8,400,128]{2,1,0:T(8,128)(2,1)} %broadcast_in_dim.89), calls=%async_computation | async-start | bytes 1638400 | tf_op jit(solution)/shard_map/while/body/eval_jaxpr/all_to_all | solution.py:21
  901.2 13.8 %all-to-all-start = ((bf16[8,400,128]{2,1,0:T(8,128)(2,1)}), bf16[8,400,128]{2,1,0:T(8,128)(2,1)S(1)}, u32[]{:S(2)}, u32[]{:S(2)}) async-start(bf16[8,400,128]{2,1,0:T(8,128)(2,1)} %broadcast_in_dim.89), calls=%async_computation | async-start | bytes 1638400 | tf_op jit(solution)/shard_map/while/body/eval_jaxpr/all_to_all | solution.py:21
  931.3 13.8 %all-to-all-start = ((bf16[8,400,128]{2,1,0:T(8,128)(2,1)}), bf16[8,400,128]{2,1,0:T(8,128)(2,1)S(1)}, u32[]{:S(2)}, u32[]{:S(2)}) async-start(bf16[8,400,128]{2,1,0:T(8,128)(2,1)} %broadcast_in_dim.89), calls=%async_computation | async-start | bytes 1638400 | tf_op jit(solution)/shard_map/while/body/eval_jaxpr/all_to_all | solution.py:21
  961.4 13.8 %all-to-all-start = ((bf16[8,400,128]{2,1,0:T(8,128)(2,1)}), bf16[8,400,128]{2,1,0:T(8,128)(2,1)S(1)}, u32[]{:S(2)}, u32[]{:S(2)}) async-start(bf16[8,400,128]{2,1,0:T(8,128)(2,1)} %broadcast_in_dim.89), calls=%async_computation | async-start | bytes 1638400 | tf_op jit(solution)/shard_map/while/body/eval_jaxpr/all_to_all | solution.py:21
  991.5 13.8 %all-to-all-start = ((bf16[8,400,128]{2,1,0:T(8,128)(2,1)}), bf16[8,400,128]{2,1,0:T(8,128)(2,1)S(1)}, u32[]{:S(2)}, u32[]{:S(2)}) async-start(bf16[8,400,128]{2,1,0:T(8,128)(2,1)} %broadcast_in_dim.89), calls=%async_computation | async-start | bytes 1638400 | tf_op jit(solution)/shard_map/while/body/eval_jaxpr/all_to_all | solution.py:21
  1021.7 13.8 %all-to-all-start = ((bf16[8,400,128]{2,1,0:T(8,128)(2,1)}), bf16[8,400,128]{2,1,0:T(8,128)(2,1)S(1)}, u32[]{:S(2)}, u32[]{:S(2)}) async-start(bf16[8,400,128]{2,1,0:T(8,128)(2,1)} %broadcast_in_dim.89), calls=%async_computation | async-start | bytes 1638400 | tf_op jit(solution)/shard_map/while/body/eval_jaxpr/all_to_all | solution.py:21
  1051.8 13.8 %all-to-all-start = ((bf16[8,400,128]{2,1,0:T(8,128)(2,1)}), bf16[8,400,128]{2,1,0:T(8,128)(2,1)S(1)}, u32[]{:S(2)}, u32[]{:S(2)}) async-start(bf16[8,400,128]{2,1,0:T(8,128)(2,1)} %broadcast_in_dim.89), calls=%async_computation | async-start | bytes 1638400 | tf_op jit(solution)/shard_map/while/body/eval_jaxpr/all_to_all | solution.py:21
  1081.9 13.8 %all-to-all-start = ((bf16[8,400,128]{2,1,0:T(8,128)(2,1)}), bf16[8,400,128]{2,1,0:T(8,128)(2,1)S(1)}, u32[]{:S(2)}, u32[]{:S(2)}) async-start(bf16[8,400,128]{2,1,0:T(8,128)(2,1)} %broadcast_in_dim.89), calls=%async_computation | async-start | bytes 1638400 | tf_op jit(solution)/shard_map/while/body/eval_jaxpr/all_to_all | solution.py:21
  1112.0 13.8 %all-to-all-start = ((bf16[8,400,128]{2,1,0:T(8,128)(2,1)}), bf16[8,400,128]{2,1,0:T(8,128)(2,1)S(1)}, u32[]{:S(2)}, u32[]{:S(2)}) async-start(bf16[8,400,128]{2,1,0:T(8,128)(2,1)} %broadcast_in_dim.89), calls=%async_computation | async-start | bytes 1638400 | tf_op jit(solution)/shard_map/while/body/eval_jaxpr/all_to_all | solution.py:21
  1142.1 13.8 %all-to-all-start = ((bf16[8,400,128]{2,1,0:T(8,128)(2,1)}), bf16[8,400,128]{2,1,0:T(8,128)(2,1)S(1)}, u32[]{:S(2)}, u32[]{:S(2)}) async-start(bf16[8,400,128]{2,1,0:T(8,128)(2,1)} %broadcast_in_dim.89), calls=%async_computation | async-start | bytes 1638400 | tf_op jit(solution)/shard_map/while/body/eval_jaxpr/all_to_all | solution.py:21
  1172.3 13.8 %all-to-all-start = ((bf16[8,400,128]{2,1,0:T(8,128)(2,1)}), bf16[8,400,128]{2,1,0:T(8,128)(2,1)S(1)}, u32[]{:S(2)}, u32[]{:S(2)}) async-start(bf16[8,400,128]{2,1,0:T(8,128)(2,1)} %broadcast_in_dim.89), calls=%async_computation | async-start | bytes 1638400 | tf_op jit(solution)/shard_map/while/body/eval_jaxpr/all_to_all | solution.py:21
  1221.2 33.3 %all-to-all-start.4 = ((bf16[8,16,8,384]{3,2,1,0:T(8,128)(2,1)}), bf16[8,16,8,384]{3,2,1,0:T(8,128)(2,1)}, u32[]{:S(2)}, u32[]{:S(2)}) async-start(bf16[8,16,8,384]{3,2,1,0:T(8,128)(2,1)} %bitcast.104), calls=%async_computation.4 | async-start | bytes 1572864 | tf_op jit(solution)/shard_map/all_to_all | solution.py:211
  (61 other events, 407.9 us)
Sparse Core Ops, SparseCore 0:
  32.9 178.0 all-gather.2

commit v2 on v1

v2 whole, which is shorter than its diff:
```python
import jax
import jax.numpy as jnp
from jax import lax
from jax.experimental import pallas as pl
from jax.experimental.pallas import tpu as pltpu
from jax.sharding import PartitionSpec as P

norm_eps = 1e-05
LANES = 128
EXTRA = 16
GROUP = 4
RING = 4
TURNS = (2, 1, 3)


def pass_down(value):
    count = lax.axis_size("section")
    return lax.ppermute(value, "section", [(source, source - 1) for source in range(1, count)])


def far_section():
    return lax.axis_size("section") // 2


def pass_near(value):
    count = lax.axis_size("section")
    pairs = [(source, source - 1) for source in range(1, count) if source != far_section()]
    return lax.ppermute(value, "section", pairs)


def pass_far(value):
    return lax.ppermute(value, "section", [(far_section(), far_section() - 1)])


def move(value, across, along):
    pairs = []
    for d in range(lax.axis_size("dp")):
        half, place = divmod(d, RING)
        pairs.append((d, (half ^ across) * RING + (place + along) % RING))
    return lax.ppermute(value, "dp", pairs)


def gather_blocks(value):
    other = move(value, 1, 0)
    own_ring = [move(value, 0, turn) for turn in TURNS]
    return [value, other] + own_ring + [move(other, 0, turn) for turn in TURNS]


def block_owners():
    half, place = lax.axis_index("dp") // RING, lax.axis_index("dp") % RING
    own_ring = [half * RING + (place + RING - turn) % RING for turn in TURNS]
    other_ring = [(1 - half) * RING + (place + RING - turn) % RING for turn in TURNS]
    return [half * RING + place, (1 - half) * RING + place] + own_ring + other_ring


def spread(value):
    count = lax.axis_size("dp")
    copies = jnp.broadcast_to(value[None], (count,) + value.shape)
    return lax.all_to_all(copies, "dp", split_axis=0, concat_axis=0, tiled=True)


def slope_of(pre_acts):
    pre_f = pre_acts.astype(jnp.float32)
    sigmoid_z = jax.nn.sigmoid(pre_f)
    return sigmoid_z * (1.0 + pre_f * (1.0 - sigmoid_z))


def split3(value):
    high = value.astype(jnp.bfloat16)
    rest = value - high.astype(jnp.float32)
    mid = rest.astype(jnp.bfloat16)
    low = (rest - mid.astype(jnp.float32)).astype(jnp.bfloat16)
    return jnp.stack([high, mid, low])


def unset(shape, dtype):
    return pl.pallas_call(
        lambda out: None,
        out_shape=jax.ShapeDtypeStruct(shape, dtype),
        out_specs=pl.BlockSpec(memory_space=pltpu.HBM),
        name="unset",
    )()


EARLY = 5


def as_columns(block, tokens, pieces):
    return jnp.concatenate([block[j * tokens : (j + 1) * tokens, :] for j in range(pieces)], axis=1)


def columns_of(info, i, cols):
    return pl.ds(pl.multiple_of(info[5 + i] * cols, LANES), cols)


def fetch_upper(info, sources, buffer, sem, start, cols=None, i=0):
    copies = []
    for source in sources:
        view = source.at[info[4]]
        if cols is not None:
            view = view.at[:, columns_of(info, i, cols)]
        copies.append(pltpu.make_async_copy(view, buffer, sem))
    if start:
        for at, copy in enumerate(copies):
            if len(copies) == 1:
                copy.start()
            else:
                pl.when(info[3] == at)(copy.start)
    return copies[0]


def products(info, blocks, first, weight_t, uppers, upper_buf, weight_buf, sems, total, tokens, cols):
    count = len(blocks)
    pieces = cols // LANES
    waits = []
    for i in range(count):
        upper = fetch_upper(info, uppers, upper_buf.at[i], sems.at[i], True, cols, first + i)
        rows = pl.ds(pl.multiple_of(info[5 + first + i] * cols, LANES), cols)
        weight = pltpu.make_async_copy(weight_t.at[rows, :], weight_buf.at[i], sems.at[count + i])
        weight.start()
        waits.append((upper, weight))
    for i in range(count):
        for copy in waits[i]:
            copy.wait()
        left = jnp.concatenate([as_columns(blocks[i], tokens, pieces), upper_buf[i]], axis=0)
        total = total + jnp.dot(left, weight_buf[i], preferred_element_type=jnp.float32)
    return total


def specs(smem, vmem, anywhere):
    return (
        [pl.BlockSpec(memory_space=pltpu.SMEM)] * smem
        + [pl.BlockSpec(memory_space=pltpu.VMEM)] * vmem
        + [pl.BlockSpec(memory_space=pltpu.HBM)] * anywhere
    )


LIMIT = pltpu.CompilerParams(vmem_limit_bytes=32 * 1024 * 1024)


def in_hbm(value):
    return pltpu.with_memory_space_constraint(value, pltpu.HBM)


def early_kernel(tokens, parts, width, upper_count):
    cols = width // parts

    def body(info, *refs):
        blocks, weight_t, uppers = refs[:EARLY], refs[EARLY], refs[EARLY + 1 : EARLY + 1 + upper_count]
        out, upper_buf, weight_buf, sems = refs[EARLY + 1 + upper_count :]
        total = jnp.zeros((2 * tokens, cols), jnp.float32)
        out[...] = products(info, blocks, 0, weight_t, uppers, upper_buf, weight_buf, sems, total, tokens, cols)

    return pl.pallas_call(
        body,
        out_shape=jax.ShapeDtypeStruct((2 * tokens, cols), jnp.float32),
        in_specs=specs(1, EARLY, 1 + upper_count),
        out_specs=pl.BlockSpec(memory_space=pltpu.VMEM),
        scratch_shapes=[
            pltpu.VMEM((EARLY, tokens, cols), jnp.bfloat16),
            pltpu.VMEM((EARLY, cols, cols), jnp.bfloat16),
            pltpu.SemaphoreType.DMA((2 * EARLY,)),
        ],
        name="early",
        cost_estimate=pl.CostEstimate(
            flops=4 * tokens * width * cols, bytes_accessed=2 * EARLY * cols * cols, transcendentals=0
        ),
        compiler_params=LIMIT,
    )


def tick_kernel(tokens, parts, width, upper_count):
    cols = width // parts
    pieces = cols // LANES
    body_rows = pieces * tokens
    rows = body_rows + EXTRA
    late = parts - EARLY
    across = (((1,), (1,)), ((), ()))
    down = (((0,), (0,)), ((), ()))

    def body(info, *refs):
        blocks = refs[:parts]
        early, part, gain, acc_in = refs[parts : parts + 4]
        weight_t, x_upper_all, x_all, scale_all, slope_all, top_all = refs[parts + 4 : parts + 10]
        uppers = refs[parts + 10 : parts + 10 + upper_count]
        part_out, acc_out, slope_out, top_out, coef_out = refs[parts + 10 + upper_count : parts + 15 + upper_count]
        upper_buf, weight_buf, x_upper, x_own, scale, sems, small_sems = refs[parts + 15 + upper_count :]
        slot, later = info[1], info[2]
        small = [
            pltpu.make_async_copy(x_upper_all.at[slot], x_upper, small_sems.at[0]),
            pltpu.make_async_copy(x_all.at[slot], x_own, small_sems.at[1]),
            pltpu.make_async_copy(scale_all.at[slot], scale, small_sems.at[2]),
            pltpu.make_async_copy(slope_all.at[later], slope_out, small_sems.at[3]),
            pltpu.make_async_copy(top_all.at[later], top_out, small_sems.at[4]),
        ]
        for copy in small:
            copy.start()
        sums = jnp.concatenate([block[body_rows:rows, :] for block in blocks], axis=0)
        coef = lax.dot_general(
            sums, jnp.ones((parts * EXTRA, LANES), jnp.bfloat16), down, preferred_element_type=jnp.float32
        )[:tokens]
        coef_out[...] = coef
        both = products(
            info, blocks[EARLY:], EARLY, weight_t, uppers, upper_buf, weight_buf, sems, early[...], tokens, cols
        )
        for copy in small[:3]:
            copy.wait()
        scale_v = scale[...]
        total = jnp.zeros((tokens, LANES), jnp.float32)
        for j in range(pieces):
            here = slice(j * tokens, (j + 1) * tokens)
            lanes = slice(j * LANES, (j + 1) * LANES)
            grad_j = both[:tokens, lanes] - coef * both[tokens:, lanes]
            x_j = x_own[here, :].astype(jnp.float32)
            scaled = gain[:, lanes] * grad_j
            incoming = part[here, :].astype(jnp.float32) - coef * x_upper[here, :].astype(jnp.float32)
            part_out[here, :] = (incoming + scale_v * scaled).astype(jnp.bfloat16)
            total = total + scaled * x_j
            gain_sum = jnp.sum(grad_j * x_j * scale_v, axis=0, keepdims=True)
            acc_out[:, lanes] = acc_in[:, lanes] + jnp.where(info[0] > 0, gain_sum, 0.0)
        total = total * (scale_v * scale_v * scale_v * (1.0 / width))
        if tokens < LANES:
            total = jnp.concatenate([total, jnp.zeros((LANES - tokens, LANES), jnp.float32)], axis=0)
        high = total.astype(jnp.bfloat16)
        low = (total - high.astype(jnp.float32)).astype(jnp.bfloat16)
        ones = jnp.ones((EXTRA, LANES), jnp.bfloat16)
        line = lax.dot_general(ones, high, across, preferred_element_type=jnp.float32)
        line = line + lax.dot_general(ones, low, across, preferred_element_type=jnp.float32)
        line_high = line.astype(jnp.bfloat16).astype(jnp.float32)
        row = lax.broadcasted_iota(jnp.int32, (EXTRA, LANES), 0)
        packed = jnp.where(row == 0, line_high, jnp.where(row == 1, line - line_high, 0.0))
        part_out[body_rows:rows, :] = packed.astype(jnp.bfloat16)
        for copy in small[3:]:
            copy.wait()

    return pl.pallas_call(
        body,
        out_shape=(
            jax.ShapeDtypeStruct((rows, LANES), jnp.bfloat16),
            jax.ShapeDtypeStruct((1, cols), jnp.float32),
            jax.ShapeDtypeStruct((rows, LANES), jnp.float32),
            jax.ShapeDtypeStruct((rows, LANES), jnp.bfloat16),
            jax.ShapeDtypeStruct((tokens, LANES), jnp.float32),
        ),
        in_specs=specs(1, parts + 4, 6 + upper_count),
        out_specs=(pl.BlockSpec(memory_space=pltpu.VMEM),) * 5,
        scratch_shapes=[
            pltpu.VMEM((late, tokens, cols), jnp.bfloat16),
            pltpu.VMEM((late, cols, cols), jnp.bfloat16),
            pltpu.VMEM((body_rows, LANES), jnp.bfloat16),
            pltpu.VMEM((body_rows, LANES), jnp.bfloat16),
            pltpu.VMEM((tokens, LANES), jnp.float32),
            pltpu.SemaphoreType.DMA((2 * late,)),
            pltpu.SemaphoreType.DMA((5,)),
        ],
        name="tick",
        cost_estimate=pl.CostEstimate(
            flops=4 * tokens * width * cols, bytes_accessed=2 * late * cols * cols, transcendentals=0
        ),
        compiler_params=LIMIT,
    )


def grads_kernel(tokens, parts, width, upper_count, slots):
    cols = width // parts
    pieces = cols // LANES

    def body(info, *refs):
        blocks, coef_ref = refs[:parts], refs[parts]
        uppers = refs[parts + 1 : parts + 1 + upper_count]
        _, store, out, upper, sem = refs[parts + 1 + upper_count :]
        copy = fetch_upper(info, uppers, upper, sem, True)
        coef = coef_ref[...]
        copy.wait()
        for i in range(parts):
            for j in range(pieces):
                at = pl.ds(pl.multiple_of(info[5 + i] * cols + j * LANES, LANES), LANES)
                piece = blocks[i][j * tokens : (j + 1) * tokens, :].astype(jnp.float32)
                out[:, at] = (piece - coef * upper[:, at].astype(jnp.float32)).astype(jnp.bfloat16)
        back = pltpu.make_async_copy(out, store.at[info[5 + parts]], sem)
        back.start()
        back.wait()

    return pl.pallas_call(
        body,
        out_shape=jax.ShapeDtypeStruct((slots, tokens, width), jnp.bfloat16),
        in_specs=specs(1, parts + 1, upper_count + 1),
        out_specs=pl.BlockSpec(memory_space=pltpu.HBM),
        input_output_aliases={parts + 2 + upper_count: 0},
        scratch_shapes=[
            pltpu.VMEM((tokens, width), jnp.bfloat16),
            pltpu.VMEM((tokens, width), jnp.bfloat16),
            pltpu.SemaphoreType.DMA,
        ],
        name="grads",
        cost_estimate=pl.CostEstimate(flops=2 * tokens * width, bytes_accessed=6 * tokens * width, transcendentals=0),
        compiler_params=LIMIT,
    )


def on_device(layer_in, pre_act, weight, gain, cot_top):
    sections = lax.axis_size("section")
    parts = lax.axis_size("dp")
    section_idx = lax.axis_index("section")
    dp_idx = lax.axis_index("dp")
    inputs = layer_in[0]
    pre_acts = pre_act[0]
    micro, own_rows, width = inputs.shape
    tokens = own_rows * parts
    cols = width // parts
    pieces = cols // LANES
    share = sections // parts
    share_pieces = pieces // share
    body_rows = pieces * tokens
    groups = micro // GROUP
    is_last = section_idx == sections - 1
    gain_cols = lax.dynamic_slice_in_dim(gain, dp_idx * cols, cols, axis=1)
    weight_rows = weight[0]
    weight_t = weight_rows.T

    def as_pieces(value, count, own):
        value = value.reshape(parts, -1, own, count, LANES)
        return value.transpose(1, 3, 0, 2, 4).reshape(-1, count * parts * own, LANES)

    def prepare(first, last, token):
        count = last - first
        local = count * own_rows
        x = inputs[first:last]
        x_f = x.astype(jnp.float32)
        side = split3(jnp.mean(x_f * x_f, axis=-1).reshape(1, local))[:, 0]
        side = jnp.pad(side, ((0, EXTRA - 3), (0, cols - local)))
        if token is not None:
            side = side + token
        ends = cot_top[first:last].reshape(local // share, cols)
        both = jnp.concatenate([side, ends], axis=0)
        message = jnp.concatenate(
            [
                pre_acts[first:last].reshape(local, parts, cols).transpose(1, 0, 2),
                x.reshape(local, parts, cols).transpose(1, 0, 2),
                jnp.broadcast_to(both[None], (parts,) + both.shape),
            ],
            axis=1,
        )
        got = lax.all_to_all(message, "dp", split_axis=0, concat_axis=0, tiled=True)
        slope = slope_of(as_pieces(got[:, :local], pieces, own_rows))
        slope = jnp.pad(slope, ((0, 0), (0, EXTRA), (0, 0)), constant_values=1.0)
        x_got = got[:, local : 2 * local]
        x_pieces = as_pieces(x_got, pieces, own_rows)
        sq = jnp.sum(got[:, 2 * local : 2 * local + 3, :local].astype(jnp.float32), axis=1)
        if token is None:
            sq = sq + weight_t[0, 0].astype(jnp.float32) * 0
        sq = sq.reshape(parts, count, own_rows).transpose(1, 0, 2).reshape(count, tokens)
        row_scale = lax.rsqrt(sq + norm_eps)[..., None]
        x_cols = x_got.reshape(parts, count, own_rows, cols).transpose(1, 0, 2, 3).reshape(count, tokens, cols)
        normed = (x_cols.astype(jnp.float32) * row_scale * gain_cols).astype(jnp.bfloat16)
        top_all = got[:, 2 * local + EXTRA :].reshape(parts, local, cols // share)
        top_all = as_pieces(top_all, share_pieces, own_rows)
        top = []
        for i in range(share):
            pairs = [(d * sections + d * share + i, d * sections + sections - 1) for d in range(parts)]
            top.append(lax.ppermute(top_all, ("dp", "section"), pairs))
        top = jnp.pad(jnp.concatenate(top, axis=1), ((0, 0), (0, EXTRA), (0, 0)))
        small = (
            pass_down(x_pieces),
            x_pieces,
            jnp.broadcast_to(row_scale, (count, tokens, LANES)),
            slope,
            top,
        )
        return small, normed, sq[0, 0].astype(jnp.bfloat16) * 0

    def upper_terms(first, token):
        here = slice(first, first + GROUP)
        upper = pass_down(inputs[here]).astype(jnp.float32) * slope_of(pre_acts[here])
        upper = upper.astype(jnp.bfloat16)
        if token is not None:
            upper = upper + token
        return lax.all_gather(upper, "dp", axis=1, tiled=True)

    owners = block_owners()

    after = (sections - 1 - section_idx) + (section_idx < far_section()).astype(jnp.int32)

    def slot_of(tick_num, count):
        return jnp.clip(tick_num - after, 0, count - 1)

    def run(first, last, small, uppers, state):
        sizes = (tokens, parts, width, len(uppers))
        early, tick = early_kernel(*sizes), tick_kernel(*sizes)
        grads = grads_kernel(*sizes, micro + 1)
        here = small[0].shape[0]
        ready = uppers[0].shape[0] * len(uppers)

        def tick_step(tick_num, state):
            near, far, newest, slope_here, top_here, grad_store, gain_acc, bottom_store = state
            far_next = pass_far(newest)
            slot_pos = tick_num - after
            is_live = (slot_pos >= 0) & (slot_pos < micro)
            slot = slot_of(tick_num, here)
            upper_slot = jnp.minimum(slot, ready - 1)
            received = jnp.where(section_idx == far_section() - 1, far, near)
            part = jnp.where(is_last, top_here, received)
            sent = (part.astype(jnp.float32) * slope_here).astype(jnp.bfloat16)
            group = uppers[0].shape[0]
            keep = jnp.where(slot_pos < micro, slot, micro)
            scalars = [is_live, slot, slot_of(tick_num + 1, here), upper_slot // group, upper_slot % group]
            info = jnp.stack([v.astype(jnp.int32) for v in scalars + owners + [keep]])
            blocks = gather_blocks(sent)
            weight_here = in_hbm(weight_t)
            uppers_here = [in_hbm(value) for value in uppers]
            small_here = [in_hbm(value) for value in small]
            early_sums = early(info, *blocks[:EARLY], weight_here, *uppers_here)
            newest, gain_acc, slope_here, top_here, coef = tick(
                info, *blocks, early_sums, part, gain_cols, gain_acc, weight_here, *small_here, *uppers_here
            )
            grad_store = grads(info, *blocks, coef, *uppers_here, in_hbm(grad_store))
            bottom_store = lax.dynamic_update_index_in_dim(bottom_store, newest, slot, 0)
            return (pass_near(newest), far_next, newest, slope_here, top_here, grad_store, gain_acc, bottom_store)

        return lax.fori_loop(first, last, tick_step, state)

    ticks = sections + micro
    small, normed, token = prepare(0, micro, None)
    uppers = [upper_terms(first, token if first else None) for first in range(0, micro, GROUP)]
    empty = jnp.zeros((body_rows + EXTRA, LANES), jnp.bfloat16)
    state = (
        empty,
        empty,
        empty,
        small[3][0],
        small[4][0],
        unset((micro + 1, tokens, width), jnp.bfloat16),
        jnp.zeros((1, cols), jnp.float32),
        unset((micro, body_rows + EXTRA, LANES), jnp.bfloat16),
    )
    state = run(0, 1, small, [weight_rows.reshape(-1, tokens, width)], state)
    state = run(1, GROUP, small, uppers[:1], state)
    for group in range(1, groups):
        last = ticks if group + 1 == groups else (group + 1) * GROUP
        state = run(group * GROUP, last, small, uppers[: group + 1], state)
    grad_store, gain_acc, bottom_store = state[5:]

    own = jnp.sum(bottom_store[:, body_rows : body_rows + 2, :tokens].astype(jnp.float32), axis=1)
    own = jnp.sum(spread(own), axis=0)
    coef = jnp.tile(own, (1, pieces))[..., None]
    bottom = bottom_store[:, :body_rows].astype(jnp.float32) - coef * small[1].astype(jnp.float32)
    bottom = bottom.astype(jnp.bfloat16)
    part_rows = share_pieces * tokens
    mine = None
    for i in range(share):
        pairs = [(d * sections, d * sections + d * share + i) for d in range(parts)]
        moved = lax.ppermute(bottom[:, i * part_rows : (i + 1) * part_rows], ("dp", "section"), pairs)
        mine = moved if mine is None else jnp.where(section_idx % share == i, moved, mine)
    weight_grad = jnp.einsum(
        "mki,mkj->ij", normed, grad_store[:micro], preferred_element_type=jnp.float32
    ).astype(jnp.bfloat16)
    mine = mine + weight_grad[0, 0] * 0
    mine = mine.reshape(micro, share_pieces, parts, own_rows, LANES).transpose(2, 0, 3, 1, 4)
    mine = mine.reshape(parts, micro, own_rows, share_pieces * LANES)
    shares = lax.all_to_all(mine, "dp", split_axis=0, concat_axis=0, tiled=True)
    own_block = lax.dynamic_index_in_dim(shares, section_idx // share, 0, keepdims=False)
    return (own_block, weight_grad[None], gain_acc)


def solution(mesh):
    return jax.shard_map(
        on_device,
        mesh=mesh,
        in_specs=(
            P("section", None, "dp", None),
            P("section", None, "dp", None),
            P("section", "dp", None),
            P("section", None),
            P(None, "dp", "section"),
        ),
        out_specs=(P(None, "dp", "section"), P("section", "dp", None), P("section", "dp")),
        check_vma=False,
    )
```

time: 1280 us -> 1140 us (0.89)
  Pallas kernels: 67.8 us -> 331 us
  waiting for transfers between devices: 358 us -> 101 us
  local copies, waits for them, and re-layouts: 300 us -> 98.5 us
  starting transfers between devices: 442 us -> 535 us
  other arithmetic: 51.5 us -> 22.6 us
    ppermute x2 -> x290, starting transfers between devices: 3.15 us -> 496 us  [the longest x224 348 us: move(): return lax.ppermute(value, 'dp', pairs)]
    ppermute x33 -> x5, starting transfers between devices: 295 us -> 15.6 us  [pass_down(): lax.ppermute(value, 'section', [(source, source - 1) for source in range(...]
    pallas_call x31 -> x98, Pallas kernels: 67.8 us -> 331 us  [the longest x32 124 us: tick_step(): early_sums = early(info, *blocks[:EARLY], weight_here, *uppers_here)]
    all_to_all x32 -> x1, waiting for transfers between devices: 258 us -> 6.31 us  [spread(): return lax.all_to_all(copies, 'dp', split_axis=0, concat_axis=0, tiled=True)]
    while x93 -> x31, local copies, waits for them, and re-layouts: 114 us -> 0.05 us
    all_to_all x32 -> x1, starting transfers between devices: 120 us -> 6.21 us  [spread(): return lax.all_to_all(copies, 'dp', split_axis=0, concat_axis=0, tiled=True)]
    reshape x31 -> x1, local copies, waits for them, and re-layouts: 36.9 us -> 0.04 us  [prepare(): ends = cot_top[first:last].reshape(local // share, cols)]
    ppermute x33 -> x5, waiting for transfers between devices: 38.5 us -> 2.01 us  [pass_down(): lax.ppermute(value, 'section', [(source, source - 1) for source in range(...]
  transfers between devices with their start and end apart: 72 -> 304, of which waited for: 66 -> 47; matrix products, arithmetic and copies ran while one was open for 13% -> 9% of each run, Pallas kernels for 0% -> 23%
where the time goes in v2:
time: 1140 us; the launch traced here: 1130 us
  starting transfers between devices  535 us (47%)
  Pallas kernels  331 us (29%)
  waiting for transfers between devices  101 us (9%)
  local copies, waits for them, and re-layouts  98.5 us (9%)
  other arithmetic  22.6 us (2%)
  matrix products  17.3 us (2%)
  between operations  16.6 us (1%)
  loops' own time  11.9 us (1%)
    ppermute x224, starting transfers between devices, move(): return lax.ppermute(value, 'dp', pairs)  348 us
    pallas_call x32, Pallas kernels, tick_step(): early_sums = early(info, *blocks[:EARLY], weight_here, *uppers_here)  124 us
    pallas_call x32, Pallas kernels, tick_step(): tick(info, *blocks, early_sums, part, gain_cols, gain_acc, weight_here, *...  116 us
    ppermute x32, starting transfers between devices, pass_far(): return lax.ppermute(value, 'section', [(far_section(), far_section() - 1)])  105 us
    pallas_call x32, Pallas kernels, tick_step(): grad_store = grads(info, *blocks, coef, *uppers_here, in_hbm(grad_store))  91.7 us
    all_to_all x1, waiting for transfers between devices, prepare(): got = lax.all_to_all(message, 'dp', split_axis=0, concat_axis=0, tiled=True)  46 us
    ppermute x32, starting transfers between devices, pass_near(): return lax.ppermute(value, 'section', pairs)  41.3 us
    ppermute x224, waiting for transfers between devices, move(): return lax.ppermute(value, 'dp', pairs)  36.1 us
  transfers between devices with their start and end apart: 304, of which 47 were waited for; matrix products, arithmetic and copies ran while one was open for 9% of the time, Pallas kernels for 23%

profile of v2, /device:TPU:64, one launch (start us, length us, event | category | flops | bytes accessed | tf_op | source)
XLA Modules:
  0.0 1134.6 jit_solution(10675581662701450424)
XLA Ops:
  25.5 6.6 all-to-all-start
  32.1 6.5 collective-permute-start.49
  42.6 12.6 %copy.67 = bf16[1,768,6144]{1,2,0:T(8,128)(2,1)} copy(bf16[1,768,6144]{2,1,0:T(8,128)(2,1)} %param.15) | data formatting | bytes 18874368 | tf_op args[2]
  57.0 46.0 %all-to-all-done = bf16[8,336,768]{2,1,0:T(8,128)(2,1)} async-done(((bf16[8,336,768]{2,1,0:T(8,128)(2,1)}), bf16[8,336,768]{2,1,0:T(8,128)(2,1)}, u32[]{:S(2)}, u32[]{:S(2)}) %all-to-all-start) | async-done | bytes 4128800 | tf_op jit(solution)/shard_map/all_to_all | solution.py:344
  110.8 5.4 convert_bitcast_fusion
  131.9 28.7 %collective-permute-start.38 = (bf16[400,128]{1,0:T(8,128)(2,1)S(1)}, bf16[400,128]{1,0:T(8,128)(2,1)S(1)}, u32[]{:S(2)}, u32[]{:S(2)}) collective-permute-start(bf16[400,128]{1,0:T(8,128)(2,1)S(1)} %get-tuple-element.4716.refs_0_), channel_id=1, source_target_pairs={{0,64},{16,80},{32,96},{48,112},{64,0},{80,16},{96,32},{112,48},{1... | collective-permute-start | bytes 307208 | tf_op jit(solution)/shard_map/while/body/eval_jaxpr/ppermute | solution.py:40
  175.1 3.9 early.5.refs_8_
  179.0 32.9 %collective-permute-start.47 = (bf16[400,128]{1,0:T(8,128)(2,1)S(1)}, bf16[400,128]{1,0:T(8,128)(2,1)S(1)}, u32[]{:S(2)}, u32[]{:S(2)}) collective-permute-start(bf16[400,128]{1,0:T(8,128)(2,1)S(1)} %select_n.468), channel_id=1, source_target_pairs={{8,7},{24,23},{40,39},{56,55},{72,71},{88,87},{104,103},{120,119}} | collective-permute-start | bytes 307208 | tf_op jit(solution)/shard_map/while/body/eval_jaxpr/ppermute | solution.py:32
  221.6 94.8 %while.140 = (s32[]{:T(128)}, bf16[400,128]{1,0:T(8,128)(2,1)S(1)}, bf16[400,128]{1,0:T(8,128)(2,1)S(1)}, bf16[400,128]{1,0:T(8,128)(2,1)S(1)}, f32[400,128]{1,0...) while((s32[]{:T(128)}, bf16[400,128]{1,0:T(8,128)(2,1)S(1)}, ...), condition=%wide.region_3.4_spmd.clone, body=%wide.region_2.3_spmd.clone.sunk | while | flops 2416961536 | bytes 16940560 | solution.py:420
  239.1 3.9 early.6.refs_8_
  253.9 4.6 collective-permute-start.8
  302.9 3.9 early.6.refs_8_
  316.4 106.3 %while.141 = (s32[]{:T(128)}, bf16[400,128]{1,0:T(8,128)(2,1)S(1)}, bf16[400,128]{1,0:T(8,128)(2,1)S(1)}, bf16[400,128]{1,0:T(8,128)(2,1)S(1)}, f32[400,128]{1,0...) while((s32[]{:T(128)}, bf16[400,128]{1,0:T(8,128)(2,1)S(1)}, ...), condition=%wide.region_5.6_spmd.clone, body=%wide.region_4.5_spmd.clone.sunk | while | flops 2416961536 | bytes 16940596 | solution.py:420
  330.6 3.9 early.7.refs_8_
  356.6 3.9 early.7.refs_8_
  383.8 3.9 early.7.refs_8_
  409.4 3.9 early.7.refs_8_
  422.7 114.7 %while.142 = (s32[]{:T(128)}, bf16[400,128]{1,0:T(8,128)(2,1)S(1)}, bf16[400,128]{1,0:T(8,128)(2,1)S(1)}, bf16[400,128]{1,0:T(8,128)(2,1)S(1)}, f32[400,128]{1,0...) while((s32[]{:T(128)}, bf16[400,128]{1,0:T(8,128)(2,1)S(1)}, ...), condition=%wide.region_7.8_spmd.clone, body=%wide.region_6.7_spmd.clone.sunk | while | flops 2416961536 | bytes 16940612 | solution.py:420
  445.3 3.9 early.8.refs_8_
  470.9 3.9 early.8.refs_8_
  498.4 3.9 early.8.refs_8_
  524.0 3.9 early.8.refs_8_
  537.4 531.1 %while.143 = (s32[]{:T(128)}, bf16[400,128]{1,0:T(8,128)(2,1)S(1)}, bf16[400,128]{1,0:T(8,128)(2,1)S(1)}, bf16[400,128]{1,0:T(8,128)(2,1)S(1)}, f32[400,128]{1,0...) while((s32[]{:T(128)}, bf16[400,128]{1,0:T(8,128)(2,1)S(1)}, ...), condition=%wide.region_9.10_spmd.clone, body=%wide.region_8.9_spmd.clone.sunk | while | flops 2416961536 | bytes 16940600 | solution.py:420
  551.5 3.9 early.9.refs_8_
  577.1 3.9 early.9.refs_8_
  604.7 3.9 early.9.refs_8_
  630.2 3.9 early.9.refs_8_
  657.9 3.9 early.9.refs_8_
  683.3 3.9 early.9.refs_8_
  710.9 3.9 early.9.refs_8_
  736.5 3.9 early.9.refs_8_
  764.1 3.9 early.9.refs_8_
  789.6 3.9 early.9.refs_8_
  817.2 3.9 early.9.refs_8_
  842.7 3.9 early.9.refs_8_
  870.3 3.9 early.9.refs_8_
  895.8 3.9 early.9.refs_8_
  923.4 3.9 early.9.refs_8_
  948.9 3.9 early.9.refs_8_
  976.5 3.9 early.9.refs_8_
  1002.0 3.9 early.9.refs_8_
  1029.6 3.9 early.9.refs_8_
  1055.1 3.9 early.9.refs_8_
  1070.0 6.2 all-to-all-start.1
  1076.2 6.3 all-to-all-done.1
  1088.1 17.3 %bitcast_convert_fusion = bf16[768,6144]{1,0:T(8,128)(2,1)} fusion(bf16[17,64,6144]{2,1,0:T(8,128)(2,1)} %get-tuple-element.3728, f32[16,8,8,768]{3,2,0,1:T(8,128)S(1)} %copy-done.6, f32[768]{0:T(1024)S(1)} %copy-done.13, f32[16,64]{1,0:T(8,128)S(1)} %get-tuple-element.6096), kind=kOutput, calls=%fused_computation.16 | convolution fusion | flops 9670754304 | bytes 25172992 | tf_op jit(solution)/shard_map/mki,mkj->ij/dot_general | solution.py:454
  1108.3 8.8 all-to-all-start.2
  1117.1 10.1 all-to-all-done.2
  (907 shorter events, 794.4 us)
Async XLA Ops:
  7.2 214.4 %all-gather.5.cloned.1.call-start = ((), (), s32[]{:S(2)}) async-start(), calls=%async_computation.3 | async-start | bytes 3538944 | tf_op jit(solution)/shard_map/all_gather | solution.py:378
  25.5 77.5 %all-to-all-start = ((bf16[8,336,768]{2,1,0:T(8,128)(2,1)}), bf16[8,336,768]{2,1,0:T(8,128)(2,1)}, u32[]{:S(2)}, u32[]{:S(2)}) async-start(bf16[8,336,768]{2,1,0:T(8,128)(2,1)} %copy.64), calls=%async_computation | async-start | bytes 8257536 | tf_op jit(solution)/shard_map/all_to_all | solution.py:344
  32.1 284.3 %all-gather.7.cloned.1.call-start = ((), (), s32[]{:S(2)}) async-start(), calls=%async_computation.4 | async-start | bytes 3538944 | tf_op jit(solution)/shard_map/all_gather | solution.py:378
  32.1 75.0 %collective-permute-start.49 = (bf16[4,8,6144]{2,1,0:T(8,128)(2,1)S(1)}, bf16[4,8,6144]{2,1,0:T(8,128)(2,1)S(1)}, u32[]{:S(2)}, u32[]{:S(2)}) collective-permute-start(bf16[4,8,6144]{2,1,0:T(8,128)(2,1)S(1)} %copy-done.10), channel_id=1, source_target_pairs={{1,0},{2,1},{3,2},{4,3},{5,4},{6,5},{7,6},{8,7},{9,8},{10,9},{11,1... | collective-permute-start | bytes 1179656 | tf_op jit(solution)/shard_map/ppermute | solution.py:18
  38.7 68.4 %collective-permute-start.50 = (bf16[4,8,6144]{2,1,0:T(8,128)(2,1)S(1)}, bf16[4,8,6144]{2,1,0:T(8,128)(2,1)S(1)}, u32[]{:S(2)}, u32[]{:S(2)}) collective-permute-start(bf16[4,8,6144]{2,1,0:T(8,128)(2,1)S(1)} %copy-done.9), channel_id=1, source_target_pairs={{1,0},{2,1},{3,2},{4,3},{5,4},{6,5},{7,6},{8,7},{9,8},{10,9},{11,1... | collective-permute-start | bytes 1179656 | tf_op jit(solution)/shard_map/ppermute | solution.py:18
  40.6 66.5 %collective-permute-start.51 = (bf16[4,8,6144]{2,1,0:T(8,128)(2,1)S(1)}, bf16[4,8,6144]{2,1,0:T(8,128)(2,1)}, u32[]{:S(2)}, u32[]{:S(2)}) collective-permute-start(bf16[4,8,6144]{2,1,0:T(8,128)(2,1)S(1)} %copy-done.8), channel_id=1, source_target_pairs={{1,0},{2,1},{3,2},{4,3},{5,4},{6,5},{7,6},{8,7},{9,8},{10,9},{11,1... | collective-permute-start | bytes 1179656 | tf_op jit(solution)/shard_map/ppermute | solution.py:18
  110.0 312.7 %all-gather.9.cloned.1.call-start = ((), (), s32[]{:S(2)}) async-start(), calls=%async_computation.5 | async-start | bytes 3538944 | tf_op jit(solution)/shard_map/all_gather | solution.py:378
  110.8 426.6 %all-gather.11.cloned.1.call-start = ((), (), s32[]{:S(2)}) async-start(), calls=%async_computation.6 | async-start | bytes 3538944 | tf_op jit(solution)/shard_map/all_gather | solution.py:378
  116.6 95.3 %collective-permute-start.45 = (bf16[16,384,128]{2,1,0:T(8,128)(2,1)S(1)}, bf16[16,384,128]{2,1,0:T(8,128)(2,1)}, u32[]{:S(2)}, u32[]{:S(2)}) collective-permute-start(bf16[16,384,128]{2,1,0:T(8,128)(2,1)S(1)} %bitcast.317), channel_id=1, source_target_pairs={{1,0},{2,1},{3,2},{4,3},{5,4},{6,5},{7,6},{8,7},{9,8},{10,9},{11,1... | collective-permute-start | bytes 4718600 | tf_op jit(solution)/shard_map/ppermute | solution.py:18
  131.9 37.3 %collective-permute-start.38 = (bf16[400,128]{1,0:T(8,128)(2,1)S(1)}, bf16[400,128]{1,0:T(8,128)(2,1)S(1)}, u32[]{:S(2)}, u32[]{:S(2)}) collective-permute-start(bf16[400,128]{1,0:T(8,128)(2,1)S(1)} %get-tuple-element.4716.refs_0_), channel_id=1, source_target_pairs={{0,64},{16,80},{32,96},{48,112},{64,0},{80,16},{96,32},{112,48},{1... | collective-permute-start | bytes 307208 | tf_op jit(solution)/shard_map/while/body/eval_jaxpr/ppermute | solution.py:40
  160.6 11.0 collective-permute-start.39
  160.6 11.0 collective-permute-start.40
  160.6 14.5 %collective-permute-start.41 = (bf16[400,128]{1,0:T(8,128)(2,1)S(1)}, bf16[400,128]{1,0:T(8,128)(2,1)S(1)}, u32[]{:S(2)}, u32[]{:S(2)}) collective-permute-start(bf16[400,128]{1,0:T(8,128)(2,1)S(1)} %get-tuple-element.4716.refs_0_), channel_id=1, source_target_pairs={{0,48},{16,0},{32,16},{48,32},{64,112},{80,64},{96,80},{112,96},{1... | collective-permute-start | bytes 307208 | tf_op jit(solution)/shard_map/while/body/eval_jaxpr/ppermute | solution.py:40
  169.2 42.7 %collective-permute-start.42 = (bf16[400,128]{1,0:T(8,128)(2,1)S(1)}, bf16[400,128]{1,0:T(8,128)(2,1)S(1)}, u32[]{:S(2)}, u32[]{:S(2)}) collective-permute-start(bf16[400,128]{1,0:T(8,128)(2,1)S(1)} %collective-permute-done.38.refs_1_), channel_id=1, source_target_pairs={{0,32},{16,48},{32,0},{48,16},{64,96},{80,112},{96,64},{112,80},{1... | collective-permute-start | bytes 307208 | tf_op jit(solution)/shard_map/while/body/eval_jaxpr/ppermute | solution.py:40
  171.6 40.3 %collective-permute-start.43 = (bf16[400,128]{1,0:T(8,128)(2,1)S(1)}, bf16[400,128]{1,0:T(8,128)(2,1)S(1)}, u32[]{:S(2)}, u32[]{:S(2)}) collective-permute-start(bf16[400,128]{1,0:T(8,128)(2,1)S(1)} %collective-permute-done.38.refs_1_), channel_id=1, source_target_pairs={{0,16},{16,32},{32,48},{48,0},{64,80},{80,96},{96,112},{112,64},{1... | collective-permute-start | bytes 307208 | tf_op jit(solution)/shard_map/while/body/eval_jaxpr/ppermute | solution.py:40
  171.7 40.3 %collective-permute-start.44 = (bf16[400,128]{1,0:T(8,128)(2,1)S(1)}, bf16[400,128]{1,0:T(8,128)(2,1)S(1)}, u32[]{:S(2)}, u32[]{:S(2)}) collective-permute-start(bf16[400,128]{1,0:T(8,128)(2,1)S(1)} %collective-permute-done.38.refs_1_), channel_id=1, source_target_pairs={{0,48},{16,0},{32,16},{48,32},{64,112},{80,64},{96,80},{112,96},{1... | collective-permute-start | bytes 307208 | tf_op jit(solution)/shard_map/while/body/eval_jaxpr/ppermute | solution.py:40
  179.0 42.5 %collective-permute-start.47 = (bf16[400,128]{1,0:T(8,128)(2,1)S(1)}, bf16[400,128]{1,0:T(8,128)(2,1)S(1)}, u32[]{:S(2)}, u32[]{:S(2)}) collective-permute-start(bf16[400,128]{1,0:T(8,128)(2,1)S(1)} %select_n.468), channel_id=1, source_target_pairs={{8,7},{24,23},{40,39},{56,55},{72,71},{88,87},{104,103},{120,119}} | collective-permute-start | bytes 307208 | tf_op jit(solution)/shard_map/while/body/eval_jaxpr/ppermute | solution.py:32
  221.6 13.2 %collective-permute-start = (bf16[400,128]{1,0:T(8,128)(2,1)S(1)}, bf16[400,128]{1,0:T(8,128)(2,1)S(1)}, u32[]{:S(2)}, u32[]{:S(2)}) collective-permute-start(bf16[400,128]{1,0:T(8,128)(2,1)S(1)} %get-tuple-element.5385.refs_0_), channel_id=1, source_target_pairs={{0,64},{16,80},{32,96},{48,112},{64,0},{80,16},{96,32},{112,48},{1... | collective-permute-start | bytes 307208 | tf_op jit(solution)/shard_map/while/body/eval_jaxpr/ppermute | solution.py:40
  224.0 10.9 collective-permute-start.8
  252.6 11.5 %collective-permute-start = (bf16[400,128]{1,0:T(8,128)(2,1)S(1)}, bf16[400,128]{1,0:T(8,128)(2,1)S(1)}, u32[]{:S(2)}, u32[]{:S(2)}) collective-permute-start(bf16[400,128]{1,0:T(8,128)(2,1)S(1)} %get-tuple-element.5385.refs_0_), channel_id=1, source_target_pairs={{0,64},{16,80},{32,96},{48,112},{64,0},{80,16},{96,32},{112,48},{1... | collective-permute-start | bytes 307208 | tf_op jit(solution)/shard_map/while/body/eval_jaxpr/ppermute | solution.py:40
  253.9 10.4 collective-permute-start.8
  260.7 9.6 collective-permute-start.2
  261.8 10.3 collective-permute-start.3
  264.1 12.2 %collective-permute-start.4 = (bf16[400,128]{1,0:T(8,128)(2,1)S(1)}, bf16[400,128]{1,0:T(8,128)(2,1)S(1)}, u32[]{:S(2)}, u32[]{:S(2)}) collective-permute-start(bf16[400,128]{1,0:T(8,128)(2,1)S(1)} %collective-permute-done.refs_1_), channel_id=1, source_target_pairs={{0,32},{16,48},{32,0},{48,16},{64,96},{80,112},{96,64},{112,80},{1... | collective-permute-start | bytes 307208 | tf_op jit(solution)/shard_map/while/body/eval_jaxpr/ppermute | solution.py:40
  264.3 12.4 %collective-permute-start.5 = (bf16[400,128]{1,0:T(8,128)(2,1)S(1)}, bf16[400,128]{1,0:T(8,128)(2,1)S(1)}, u32[]{:S(2)}, u32[]{:S(2)}) collective-permute-start(bf16[400,128]{1,0:T(8,128)(2,1)S(1)} %collective-permute-done.refs_1_), channel_id=1, source_target_pairs={{0,16},{16,32},{32,48},{48,0},{64,80},{80,96},{96,112},{112,64},{1... | collective-permute-start | bytes 307208 | tf_op jit(solution)/shard_map/while/body/eval_jaxpr/ppermute | solution.py:40
  267.7 11.9 %collective-permute-start.6 = (bf16[400,128]{1,0:T(8,128)(2,1)S(1)}, bf16[400,128]{1,0:T(8,128)(2,1)S(1)}, u32[]{:S(2)}, u32[]{:S(2)}) collective-permute-start(bf16[400,128]{1,0:T(8,128)(2,1)S(1)} %collective-permute-done.refs_1_), channel_id=1, source_target_pairs={{0,48},{16,0},{32,16},{48,32},{64,112},{80,64},{96,80},{112,96},{1... | collective-permute-start | bytes 307208 | tf_op jit(solution)/shard_map/while/body/eval_jaxpr/ppermute | solution.py:40
  374.2 9.6 collective-permute-start.11
  377.5 10.1 collective-permute-start.13
  439.1 10.0 collective-permute-start.22
  488.8 9.6 collective-permute-start.20
  492.2 10.1 collective-permute-start.22
  541.9 9.6 collective-permute-start.29
  545.3 10.1 collective-permute-start.31
  595.1 9.6 collective-permute-start.29
  598.4 10.1 collective-permute-start.31
  648.2 9.6 collective-permute-start.29
  651.6 10.1 collective-permute-start.31
  704.7 10.1 collective-permute-start.31
  758.0 9.9 collective-permute-start.31
  811.0 10.0 collective-permute-start.31
  864.1 10.1 collective-permute-start.31
  917.2 10.1 collective-permute-start.31
  970.3 10.1 collective-permute-start.31
  1023.4 10.1 collective-permute-start.31
  1070.0 12.5 %all-to-all-start.1 = ((f32[8,1,1024]{2,1,0:T(1,128)}), f32[8,1,1024]{2,1,0:T(1,128)S(1)}, u32[]{:S(2)}, u32[]{:S(2)}) async-start(f32[8,1,1024]{2,1,0:T(1,128)} %reshape.181), calls=%async_computation.1 | async-start | bytes 65536 | tf_op jit(solution)/shard_map/all_to_all | solution.py:59
  1086.6 20.6 %collective-permute-start.52 = (bf16[16,192,128]{2,1,0:T(8,128)(2,1)S(1)}, bf16[16,192,128]{2,1,0:T(8,128)(2,1)S(1)}, u32[]{:S(2)}, u32[]{:S(2)}) collective-permute-start(bf16[16,192,128]{2,1,0:T(8,128)(2,1)S(1)} %get-tuple-element.4722), channel_id=1, source_target_pairs={{0,1},{16,19},{32,37},{48,55},{64,73},{80,91},{96,109},{112,127}} | collective-permute-start | bytes 2359304 | tf_op jit(solution)/shard_map/ppermute | solution.py:452
  1087.3 19.9 %collective-permute-start.53 = (bf16[16,192,128]{2,1,0:T(8,128)(2,1)S(1)}, bf16[16,192,128]{2,1,0:T(8,128)(2,1)S(1)}, u32[]{:S(2)}, u32[]{:S(2)}) collective-permute-start(bf16[16,192,128]{2,1,0:T(8,128)(2,1)S(1)} %get-tuple-element.4721), channel_id=1, source_target_pairs={{0,0},{16,18},{32,36},{48,54},{64,72},{80,90},{96,108},{112,126}} | collective-permute-start | bytes 2359304 | tf_op jit(solution)/shard_map/ppermute | solution.py:452
  1108.3 18.9 %all-to-all-start.2 = ((bf16[8,16,8,384]{3,2,1,0:T(8,128)(2,1)}), bf16[8,16,8,384]{3,2,1,0:T(8,128)(2,1)S(1)}, u32[]{:S(2)}, u32[]{:S(2)}) async-start(bf16[8,16,8,384]{3,2,1,0:T(8,128)(2,1)} %bitcast.191), calls=%async_computation.2 | async-start | bytes 1572864 | tf_op jit(solution)/shard_map/all_to_all | solution.py:460
  (270 other events, 2010.4 us)
Sparse Core Ops, SparseCore 0:
  20.9 105.9 all-gather.4
  128.6 55.4 all-gather.6
  185.7 47.3 all-gather.8
  234.6 61.6 all-gather.10

commit v3 on v2

--- a/solution.py
+++ b/solution.py
@@ -268,8 +268,10 @@
     def body(info, *refs):
         blocks, coef_ref = refs[:parts], refs[parts]
         uppers = refs[parts + 1 : parts + 1 + upper_count]
-        _, store, out, upper, sem = refs[parts + 1 + upper_count :]
+        newest, _, _, store, bottom, out, upper, sem, bottom_sem = refs[parts + 1 + upper_count :]
         copy = fetch_upper(info, uppers, upper, sem, True)
+        keep_newest = pltpu.make_async_copy(newest, bottom.at[info[1]], bottom_sem)
+        keep_newest.start()
         coef = coef_ref[...]
         copy.wait()
         for i in range(parts):
@@ -280,16 +282,21 @@
         back = pltpu.make_async_copy(out, store.at[info[5 + parts]], sem)
         back.start()
         back.wait()
+        keep_newest.wait()
 
     return pl.pallas_call(
         body,
-        out_shape=jax.ShapeDtypeStruct((slots, tokens, width), jnp.bfloat16),
-        in_specs=specs(1, parts + 1, upper_count + 1),
-        out_specs=pl.BlockSpec(memory_space=pltpu.HBM),
-        input_output_aliases={parts + 2 + upper_count: 0},
+        out_shape=(
+            jax.ShapeDtypeStruct((slots, tokens, width), jnp.bfloat16),
+            jax.ShapeDtypeStruct((slots - 1, pieces * tokens + EXTRA, LANES), jnp.bfloat16),
+        ),
+        in_specs=specs(1, parts + 1, upper_count) + specs(0, 1, 2),
+        out_specs=(pl.BlockSpec(memory_space=pltpu.HBM),) * 2,
+        input_output_aliases={parts + 3 + upper_count: 0, parts + 4 + upper_count: 1},
         scratch_shapes=[
             pltpu.VMEM((tokens, width), jnp.bfloat16),
             pltpu.VMEM((tokens, width), jnp.bfloat16),
+            pltpu.SemaphoreType.DMA,
             pltpu.SemaphoreType.DMA,
         ],
         name="grads",
@@ -363,7 +370,7 @@
         small = (
             pass_down(x_pieces),
             x_pieces,
-            jnp.broadcast_to(row_scale, (count, tokens, LANES)),
+            lax.optimization_barrier(jnp.broadcast_to(row_scale, (count, tokens, LANES))),
             slope,
             top,
         )
@@ -413,8 +420,9 @@
             newest, gain_acc, slope_here, top_here, coef = tick(
                 info, *blocks, early_sums, part, gain_cols, gain_acc, weight_here, *small_here, *uppers_here
             )
-            grad_store = grads(info, *blocks, coef, *uppers_here, in_hbm(grad_store))
-            bottom_store = lax.dynamic_update_index_in_dim(bottom_store, newest, slot, 0)
+            grad_store, bottom_store = grads(
+                info, *blocks, coef, *uppers_here, newest, in_hbm(grad_store), in_hbm(bottom_store)
+            )
             return (pass_near(newest), far_next, newest, slope_here, top_here, grad_store, gain_acc, bottom_store)
 
         return lax.fori_loop(first, last, tick_step, state)

time: 1140 us -> 1070 us (0.939)
  local copies, waits for them, and re-layouts: 98.5 us -> 43.2 us
  starting transfers between devices: 535 us -> 508 us
    broadcast_in_dim x32 -> x1, local copies, waits for them, and re-layouts: 32.1 us -> 1.03 us  [prepare(): jnp.broadcast_to(row_scale, (count, tokens, LANES))]
    dynamic_update_slice x32 -> x0, local copies, waits for them, and re-layouts: 20.8 us -> none  [tick_step(): lax.dynamic_update_index_in_dim(bottom_store, newest, slot, 0)]
    ppermute x224, starting transfers between devices: 348 us -> 335 us  [move(): return lax.ppermute(value, 'dp', pairs)]
    ppermute x32, starting transfers between devices: 105 us -> 93.1 us  [pass_far(): return lax.ppermute(value, 'section', [(far_section(), far_section() - 1)])]
  transfers between devices with their start and end apart: 304 -> 304, of which waited for: 47 -> 49; matrix products, arithmetic and copies ran while one was open for 9% -> 7% of each run, Pallas kernels for 23% -> 32%
where the time goes in v3:
time: 1070 us; the launch traced here: 1050 us
  starting transfers between devices  508 us (47%)
  Pallas kernels  334 us (31%)
  waiting for transfers between devices  107 us (10%)
  local copies, waits for them, and re-layouts  43.2 us (4%)
  other arithmetic  22.7 us (2%)
  matrix products  17.3 us (2%)
  between operations  16.9 us (2%)
    ppermute x224, starting transfers between devices, move(): return lax.ppermute(value, 'dp', pairs)  335 us
    pallas_call x32, Pallas kernels, tick_step(): early_sums = early(info, *blocks[:EARLY], weight_here, *uppers_here)  124 us
    pallas_call x32, Pallas kernels, tick_step(): tick(info, *blocks, early_sums, part, gain_cols, gain_acc, weight_here, *...  117 us
    pallas_call x32, Pallas kernels, tick_step(): grads(info, *blocks, coef, *uppers_here, newest, in_hbm(grad_store), in_h...  93.6 us
    ppermute x32, starting transfers between devices, pass_far(): return lax.ppermute(value, 'section', [(far_section(), far_section() - 1)])  93.1 us
    all_to_all x1, waiting for transfers between devices, prepare(): got = lax.all_to_all(message, 'dp', split_axis=0, concat_axis=0, tiled=True)  46 us
    ppermute x224, waiting for transfers between devices, move(): return lax.ppermute(value, 'dp', pairs)  41.8 us
    ppermute x32, starting transfers between devices, pass_near(): return lax.ppermute(value, 'section', pairs)  41.3 us
  transfers between devices with their start and end apart: 304, of which 49 were waited for; matrix products, arithmetic and copies ran while one was open for 7% of the time, Pallas kernels for 32%

profile of v3, /device:TPU:64, one launch (start us, length us, event | category | flops | bytes accessed | tf_op | source)
XLA Modules:
  0.0 1054.6 jit_solution(8967532177710487233)
XLA Ops:
  25.5 6.6 all-to-all-start
  32.1 6.5 collective-permute-start.49
  42.6 12.6 %copy.60 = bf16[1,768,6144]{1,2,0:T(8,128)(2,1)} copy(bf16[1,768,6144]{2,1,0:T(8,128)(2,1)} %param.15) | data formatting | bytes 18874368 | tf_op args[2]
  57.0 46.0 %all-to-all-done = bf16[8,336,768]{2,1,0:T(8,128)(2,1)} async-done(((bf16[8,336,768]{2,1,0:T(8,128)(2,1)}), bf16[8,336,768]{2,1,0:T(8,128)(2,1)}, u32[]{:S(2)}, u32[]{:S(2)}) %all-to-all-start) | async-done | bytes 4128800 | tf_op jit(solution)/shard_map/all_to_all | solution.py:351
  110.8 5.4 convert_bitcast_fusion
  128.1 32.2 %collective-permute-start.38 = (bf16[400,128]{1,0:T(8,128)(2,1)S(1)}, bf16[400,128]{1,0:T(8,128)(2,1)S(1)}, u32[]{:S(2)}, u32[]{:S(2)}) collective-permute-start(bf16[400,128]{1,0:T(8,128)(2,1)S(1)} %get-tuple-element.4039.refs_0_), channel_id=1, source_target_pairs={{0,64},{16,80},{32,96},{48,112},{64,0},{80,16},{96,32},{112,48},{1... | collective-permute-start | bytes 307208 | tf_op jit(solution)/shard_map/while/body/eval_jaxpr/ppermute | solution.py:40
  175.7 3.9 early.5.refs_8_
  179.6 31.5 %collective-permute-start.47 = (bf16[400,128]{1,0:T(8,128)(2,1)S(1)}, bf16[400,128]{1,0:T(8,128)(2,1)S(1)}, u32[]{:S(2)}, u32[]{:S(2)}) collective-permute-start(bf16[400,128]{1,0:T(8,128)(2,1)S(1)} %select_n.453), channel_id=1, source_target_pairs={{8,7},{24,23},{40,39},{56,55},{72,71},{88,87},{104,103},{120,119}} | collective-permute-start | bytes 307208 | tf_op jit(solution)/shard_map/while/body/eval_jaxpr/ppermute | solution.py:32
  219.2 89.3 %while.136 = (s32[]{:T(128)}, bf16[400,128]{1,0:T(8,128)(2,1)S(1)}, bf16[400,128]{1,0:T(8,128)(2,1)S(1)}, bf16[400,128]{1,0:T(8,128)(2,1)S(1)}, f32[400,128]{1,0...) while((s32[]{:T(128)}, bf16[400,128]{1,0:T(8,128)(2,1)S(1)}, ...), condition=%wide.region_3.4_spmd, body=%wide.region_2.3_spmd.sunk | while | flops 2416961536 | bytes 16411665 | solution.py:428
  225.8 6.2 collective-permute-start.8
  235.5 3.9 early.6.refs_8_
  254.0 6.8 collective-permute-start.8
  264.4 3.9 early.6.refs_8_
  285.7 5.8 collective-permute-start.8
  308.6 101.9 %while.137 = (s32[]{:T(128)}, bf16[400,128]{1,0:T(8,128)(2,1)S(1)}, bf16[400,128]{1,0:T(8,128)(2,1)S(1)}, bf16[400,128]{1,0:T(8,128)(2,1)S(1)}, f32[400,128]{1,0...) while((s32[]{:T(128)}, bf16[400,128]{1,0:T(8,128)(2,1)S(1)}, ...), condition=%wide.region_5.6_spmd, body=%wide.region_4.5_spmd.sunk | while | flops 2416961536 | bytes 16411693 | solution.py:428
  315.4 6.3 collective-permute-start.17
  325.6 3.9 early.7.refs_8_
  374.0 3.9 early.7.refs_8_
  410.5 96.8 %while.138 = (s32[]{:T(128)}, bf16[400,128]{1,0:T(8,128)(2,1)S(1)}, bf16[400,128]{1,0:T(8,128)(2,1)S(1)}, bf16[400,128]{1,0:T(8,128)(2,1)S(1)}, f32[400,128]{1,0...) while((s32[]{:T(128)}, bf16[400,128]{1,0:T(8,128)(2,1)S(1)}, ...), condition=%wide.region_7.8_spmd, body=%wide.region_6.7_spmd.sunk | while | flops 2416961536 | bytes 16411709 | solution.py:428
  422.4 3.9 early.8.refs_8_
  447.2 3.9 early.8.refs_8_
  470.7 3.9 early.8.refs_8_
  495.5 3.9 early.8.refs_8_
  507.4 483.3 %while.139 = (s32[]{:T(128)}, bf16[400,128]{1,0:T(8,128)(2,1)S(1)}, bf16[400,128]{1,0:T(8,128)(2,1)S(1)}, bf16[400,128]{1,0:T(8,128)(2,1)S(1)}, f32[400,128]{1,0...) while((s32[]{:T(128)}, bf16[400,128]{1,0:T(8,128)(2,1)S(1)}, ...), condition=%wide.region_9.10_spmd, body=%wide.region_8.9_spmd.sunk | while | flops 2416961536 | bytes 16411697 | solution.py:428
  519.1 3.9 early.9.refs_8_
  543.9 3.9 early.9.refs_8_
  567.4 3.9 early.9.refs_8_
  592.3 3.9 early.9.refs_8_
  615.8 3.9 early.9.refs_8_
  640.6 3.9 early.9.refs_8_
  664.1 3.9 early.9.refs_8_
  688.9 3.9 early.9.refs_8_
  712.4 3.9 early.9.refs_8_
  737.4 3.9 early.9.refs_8_
  760.9 3.9 early.9.refs_8_
  785.7 3.9 early.9.refs_8_
  809.2 3.9 early.9.refs_8_
  834.0 3.9 early.9.refs_8_
  857.5 3.9 early.9.refs_8_
  882.4 3.9 early.9.refs_8_
  905.8 3.9 early.9.refs_8_
  930.6 3.9 early.9.refs_8_
  954.1 3.9 early.9.refs_8_
  978.9 3.9 early.9.refs_8_
  996.0 6.3 all-to-all-done.1
  1007.8 17.3 %bitcast_convert_fusion = bf16[768,6144]{1,0:T(8,128)(2,1)} fusion(bf16[17,64,6144]{2,1,0:T(8,128)(2,1)} %get-tuple-element.3791, f32[16,8,8,768]{3,2,0,1:T(8,128)S(1)} %copy-done.6, f32[768]{0:T(1024)S(1)} %copy-done.15, f32[16,64]{1,0:T(8,128)S(1)} %copy-done.13), kind=kOutput, calls=%fused_computation.8 | convolution fusion | flops 9670754304 | bytes 25172992 | tf_op jit(solution)/shard_map/mki,mkj->ij/dot_general | solution.py:462
  1028.2 8.7 all-to-all-start.2
  1036.9 10.1 all-to-all-done.2
  (879 shorter events, 711.8 us)
Async XLA Ops:
  7.2 212.0 %all-gather.5.cloned.1.call-start = ((), (), s32[]{:S(2)}) async-start(), calls=%async_computation.3 | async-start | bytes 3538944 | tf_op jit(solution)/shard_map/all_gather | solution.py:385
  25.5 77.5 %all-to-all-start = ((bf16[8,336,768]{2,1,0:T(8,128)(2,1)}), bf16[8,336,768]{2,1,0:T(8,128)(2,1)}, u32[]{:S(2)}, u32[]{:S(2)}) async-start(bf16[8,336,768]{2,1,0:T(8,128)(2,1)} %copy.57), calls=%async_computation | async-start | bytes 8257536 | tf_op jit(solution)/shard_map/all_to_all | solution.py:351
  32.1 276.5 %all-gather.7.cloned.1.call-start = ((), (), s32[]{:S(2)}) async-start(), calls=%async_computation.4 | async-start | bytes 3538944 | tf_op jit(solution)/shard_map/all_gather | solution.py:385
  32.1 75.0 %collective-permute-start.49 = (bf16[4,8,6144]{2,1,0:T(8,128)(2,1)S(1)}, bf16[4,8,6144]{2,1,0:T(8,128)(2,1)S(1)}, u32[]{:S(2)}, u32[]{:S(2)}) collective-permute-start(bf16[4,8,6144]{2,1,0:T(8,128)(2,1)S(1)} %copy-done.10), channel_id=1, source_target_pairs={{1,0},{2,1},{3,2},{4,3},{5,4},{6,5},{7,6},{8,7},{9,8},{10,9},{11,1... | collective-permute-start | bytes 1179656 | tf_op jit(solution)/shard_map/ppermute | solution.py:18
  38.7 68.4 %collective-permute-start.50 = (bf16[4,8,6144]{2,1,0:T(8,128)(2,1)S(1)}, bf16[4,8,6144]{2,1,0:T(8,128)(2,1)S(1)}, u32[]{:S(2)}, u32[]{:S(2)}) collective-permute-start(bf16[4,8,6144]{2,1,0:T(8,128)(2,1)S(1)} %copy-done.9), channel_id=1, source_target_pairs={{1,0},{2,1},{3,2},{4,3},{5,4},{6,5},{7,6},{8,7},{9,8},{10,9},{11,1... | collective-permute-start | bytes 1179656 | tf_op jit(solution)/shard_map/ppermute | solution.py:18
  40.6 66.5 %collective-permute-start.51 = (bf16[4,8,6144]{2,1,0:T(8,128)(2,1)S(1)}, bf16[4,8,6144]{2,1,0:T(8,128)(2,1)}, u32[]{:S(2)}, u32[]{:S(2)}) collective-permute-start(bf16[4,8,6144]{2,1,0:T(8,128)(2,1)S(1)} %copy-done.8), channel_id=1, source_target_pairs={{1,0},{2,1},{3,2},{4,3},{5,4},{6,5},{7,6},{8,7},{9,8},{10,9},{11,1... | collective-permute-start | bytes 1179656 | tf_op jit(solution)/shard_map/ppermute | solution.py:18
  110.0 300.5 %all-gather.9.cloned.1.call-start = ((), (), s32[]{:S(2)}) async-start(), calls=%async_computation.5 | async-start | bytes 3538944 | tf_op jit(solution)/shard_map/all_gather | solution.py:385
  110.8 396.6 %all-gather.11.cloned.1.call-start = ((), (), s32[]{:S(2)}) async-start(), calls=%async_computation.6 | async-start | bytes 3538944 | tf_op jit(solution)/shard_map/all_gather | solution.py:385
  116.7 94.5 %collective-permute-start.45 = (bf16[16,384,128]{2,1,0:T(8,128)(2,1)S(1)}, bf16[16,384,128]{2,1,0:T(8,128)(2,1)}, u32[]{:S(2)}, u32[]{:S(2)}) collective-permute-start(bf16[16,384,128]{2,1,0:T(8,128)(2,1)S(1)} %bitcast.299), channel_id=1, source_target_pairs={{1,0},{2,1},{3,2},{4,3},{5,4},{6,5},{7,6},{8,7},{9,8},{10,9},{11,1... | collective-permute-start | bytes 4718600 | tf_op jit(solution)/shard_map/ppermute | solution.py:18
  128.1 41.8 %collective-permute-start.38 = (bf16[400,128]{1,0:T(8,128)(2,1)S(1)}, bf16[400,128]{1,0:T(8,128)(2,1)S(1)}, u32[]{:S(2)}, u32[]{:S(2)}) collective-permute-start(bf16[400,128]{1,0:T(8,128)(2,1)S(1)} %get-tuple-element.4039.refs_0_), channel_id=1, source_target_pairs={{0,64},{16,80},{32,96},{48,112},{64,0},{80,16},{96,32},{112,48},{1... | collective-permute-start | bytes 307208 | tf_op jit(solution)/shard_map/while/body/eval_jaxpr/ppermute | solution.py:40
  160.3 15.4 %collective-permute-start.41 = (bf16[400,128]{1,0:T(8,128)(2,1)S(1)}, bf16[400,128]{1,0:T(8,128)(2,1)S(1)}, u32[]{:S(2)}, u32[]{:S(2)}) collective-permute-start(bf16[400,128]{1,0:T(8,128)(2,1)S(1)} %get-tuple-element.4039.refs_0_), channel_id=1, source_target_pairs={{0,48},{16,0},{32,16},{48,32},{64,112},{80,64},{96,80},{112,96},{1... | collective-permute-start | bytes 307208 | tf_op jit(solution)/shard_map/while/body/eval_jaxpr/ppermute | solution.py:40
  169.9 41.2 %collective-permute-start.42 = (bf16[400,128]{1,0:T(8,128)(2,1)S(1)}, bf16[400,128]{1,0:T(8,128)(2,1)S(1)}, u32[]{:S(2)}, u32[]{:S(2)}) collective-permute-start(bf16[400,128]{1,0:T(8,128)(2,1)S(1)} %collective-permute-done.38.refs_1_), channel_id=1, source_target_pairs={{0,32},{16,48},{32,0},{48,16},{64,96},{80,112},{96,64},{112,80},{1... | collective-permute-start | bytes 307208 | tf_op jit(solution)/shard_map/while/body/eval_jaxpr/ppermute | solution.py:40
  172.3 38.8 %collective-permute-start.43 = (bf16[400,128]{1,0:T(8,128)(2,1)S(1)}, bf16[400,128]{1,0:T(8,128)(2,1)S(1)}, u32[]{:S(2)}, u32[]{:S(2)}) collective-permute-start(bf16[400,128]{1,0:T(8,128)(2,1)S(1)} %collective-permute-done.38.refs_1_), channel_id=1, source_target_pairs={{0,16},{16,32},{32,48},{48,0},{64,80},{80,96},{96,112},{112,64},{1... | collective-permute-start | bytes 307208 | tf_op jit(solution)/shard_map/while/body/eval_jaxpr/ppermute | solution.py:40
  172.3 38.8 %collective-permute-start.44 = (bf16[400,128]{1,0:T(8,128)(2,1)S(1)}, bf16[400,128]{1,0:T(8,128)(2,1)S(1)}, u32[]{:S(2)}, u32[]{:S(2)}) collective-permute-start(bf16[400,128]{1,0:T(8,128)(2,1)S(1)} %collective-permute-done.38.refs_1_), channel_id=1, source_target_pairs={{0,48},{16,0},{32,16},{48,32},{64,112},{80,64},{96,80},{112,96},{1... | collective-permute-start | bytes 307208 | tf_op jit(solution)/shard_map/while/body/eval_jaxpr/ppermute | solution.py:40
  179.6 39.6 %collective-permute-start.47 = (bf16[400,128]{1,0:T(8,128)(2,1)S(1)}, bf16[400,128]{1,0:T(8,128)(2,1)S(1)}, u32[]{:S(2)}, u32[]{:S(2)}) collective-permute-start(bf16[400,128]{1,0:T(8,128)(2,1)S(1)} %select_n.453), channel_id=1, source_target_pairs={{8,7},{24,23},{40,39},{56,55},{72,71},{88,87},{104,103},{120,119}} | collective-permute-start | bytes 307208 | tf_op jit(solution)/shard_map/while/body/eval_jaxpr/ppermute | solution.py:32
  225.8 18.7 %collective-permute-start.8 = (bf16[400,128]{1,0:T(8,128)(2,1)S(1)}, bf16[400,128]{1,0:T(8,128)(2,1)S(1)}, u32[]{:S(2)}, u32[]{:S(2)}) collective-permute-start(bf16[400,128]{1,0:T(8,128)(2,1)S(1)} %get-tuple-element.4881), channel_id=1, source_target_pairs={{8,7},{24,23},{40,39},{56,55},{72,71},{88,87},{104,103},{120,119}} | collective-permute-start | bytes 307208 | tf_op jit(solution)/shard_map/while/body/eval_jaxpr/ppermute | solution.py:32
  254.0 21.6 %collective-permute-start.8 = (bf16[400,128]{1,0:T(8,128)(2,1)S(1)}, bf16[400,128]{1,0:T(8,128)(2,1)S(1)}, u32[]{:S(2)}, u32[]{:S(2)}) collective-permute-start(bf16[400,128]{1,0:T(8,128)(2,1)S(1)} %get-tuple-element.4881), channel_id=1, source_target_pairs={{8,7},{24,23},{40,39},{56,55},{72,71},{88,87},{104,103},{120,119}} | collective-permute-start | bytes 307208 | tf_op jit(solution)/shard_map/while/body/eval_jaxpr/ppermute | solution.py:32
  285.7 19.9 %collective-permute-start.8 = (bf16[400,128]{1,0:T(8,128)(2,1)S(1)}, bf16[400,128]{1,0:T(8,128)(2,1)S(1)}, u32[]{:S(2)}, u32[]{:S(2)}) collective-permute-start(bf16[400,128]{1,0:T(8,128)(2,1)S(1)} %get-tuple-element.4881), channel_id=1, source_target_pairs={{8,7},{24,23},{40,39},{56,55},{72,71},{88,87},{104,103},{120,119}} | collective-permute-start | bytes 307208 | tf_op jit(solution)/shard_map/while/body/eval_jaxpr/ppermute | solution.py:32
  315.4 19.0 %collective-permute-start.17 = (bf16[400,128]{1,0:T(8,128)(2,1)S(1)}, bf16[400,128]{1,0:T(8,128)(2,1)S(1)}, u32[]{:S(2)}, u32[]{:S(2)}) collective-permute-start(bf16[400,128]{1,0:T(8,128)(2,1)S(1)} %get-tuple-element.4992), channel_id=1, source_target_pairs={{8,7},{24,23},{40,39},{56,55},{72,71},{88,87},{104,103},{120,119}} | collective-permute-start | bytes 307208 | tf_op jit(solution)/shard_map/while/body/eval_jaxpr/ppermute | solution.py:32
  344.7 14.7 %collective-permute-start.17 = (bf16[400,128]{1,0:T(8,128)(2,1)S(1)}, bf16[400,128]{1,0:T(8,128)(2,1)S(1)}, u32[]{:S(2)}, u32[]{:S(2)}) collective-permute-start(bf16[400,128]{1,0:T(8,128)(2,1)S(1)} %get-tuple-element.4992), channel_id=1, source_target_pairs={{8,7},{24,23},{40,39},{56,55},{72,71},{88,87},{104,103},{120,119}} | collective-permute-start | bytes 307208 | tf_op jit(solution)/shard_map/while/body/eval_jaxpr/ppermute | solution.py:32
  392.7 14.8 %collective-permute-start.17 = (bf16[400,128]{1,0:T(8,128)(2,1)S(1)}, bf16[400,128]{1,0:T(8,128)(2,1)S(1)}, u32[]{:S(2)}, u32[]{:S(2)}) collective-permute-start(bf16[400,128]{1,0:T(8,128)(2,1)S(1)} %get-tuple-element.4992), channel_id=1, source_target_pairs={{8,7},{24,23},{40,39},{56,55},{72,71},{88,87},{104,103},{120,119}} | collective-permute-start | bytes 307208 | tf_op jit(solution)/shard_map/while/body/eval_jaxpr/ppermute | solution.py:32
  416.5 14.8 %collective-permute-start.26 = (bf16[400,128]{1,0:T(8,128)(2,1)S(1)}, bf16[400,128]{1,0:T(8,128)(2,1)S(1)}, u32[]{:S(2)}, u32[]{:S(2)}) collective-permute-start(bf16[400,128]{1,0:T(8,128)(2,1)S(1)} %get-tuple-element.5111), channel_id=1, source_target_pairs={{8,7},{24,23},{40,39},{56,55},{72,71},{88,87},{104,103},{120,119}} | collective-permute-start | bytes 307208 | tf_op jit(solution)/shard_map/while/body/eval_jaxpr/ppermute | solution.py:32
  441.2 14.9 %collective-permute-start.26 = (bf16[400,128]{1,0:T(8,128)(2,1)S(1)}, bf16[400,128]{1,0:T(8,128)(2,1)S(1)}, u32[]{:S(2)}, u32[]{:S(2)}) collective-permute-start(bf16[400,128]{1,0:T(8,128)(2,1)S(1)} %get-tuple-element.5111), channel_id=1, source_target_pairs={{8,7},{24,23},{40,39},{56,55},{72,71},{88,87},{104,103},{120,119}} | collective-permute-start | bytes 307208 | tf_op jit(solution)/shard_map/while/body/eval_jaxpr/ppermute | solution.py:32
  464.7 14.8 %collective-permute-start.26 = (bf16[400,128]{1,0:T(8,128)(2,1)S(1)}, bf16[400,128]{1,0:T(8,128)(2,1)S(1)}, u32[]{:S(2)}, u32[]{:S(2)}) collective-permute-start(bf16[400,128]{1,0:T(8,128)(2,1)S(1)} %get-tuple-element.5111), channel_id=1, source_target_pairs={{8,7},{24,23},{40,39},{56,55},{72,71},{88,87},{104,103},{120,119}} | collective-permute-start | bytes 307208 | tf_op jit(solution)/shard_map/while/body/eval_jaxpr/ppermute | solution.py:32
  489.5 14.9 %collective-permute-start.26 = (bf16[400,128]{1,0:T(8,128)(2,1)S(1)}, bf16[400,128]{1,0:T(8,128)(2,1)S(1)}, u32[]{:S(2)}, u32[]{:S(2)}) collective-permute-start(bf16[400,128]{1,0:T(8,128)(2,1)S(1)} %get-tuple-element.5111), channel_id=1, source_target_pairs={{8,7},{24,23},{40,39},{56,55},{72,71},{88,87},{104,103},{120,119}} | collective-permute-start | bytes 307208 | tf_op jit(solution)/shard_map/while/body/eval_jaxpr/ppermute | solution.py:32
  513.1 14.8 %collective-permute-start.35 = (bf16[400,128]{1,0:T(8,128)(2,1)S(1)}, bf16[400,128]{1,0:T(8,128)(2,1)S(1)}, u32[]{:S(2)}, u32[]{:S(2)}) collective-permute-start(bf16[400,128]{1,0:T(8,128)(2,1)S(1)} %get-tuple-element.5234), channel_id=1, source_target_pairs={{8,7},{24,23},{40,39},{56,55},{72,71},{88,87},{104,103},{120,119}} | collective-permute-start | bytes 307208 | tf_op jit(solution)/shard_map/while/body/eval_jaxpr/ppermute | solution.py:32
  537.9 14.9 %collective-permute-start.35 = (bf16[400,128]{1,0:T(8,128)(2,1)S(1)}, bf16[400,128]{1,0:T(8,128)(2,1)S(1)}, u32[]{:S(2)}, u32[]{:S(2)}) collective-permute-start(bf16[400,128]{1,0:T(8,128)(2,1)S(1)} %get-tuple-element.5234), channel_id=1, source_target_pairs={{8,7},{24,23},{40,39},{56,55},{72,71},{88,87},{104,103},{120,119}} | collective-permute-start | bytes 307208 | tf_op jit(solution)/shard_map/while/body/eval_jaxpr/ppermute | solution.py:32
  561.4 14.8 %collective-permute-start.35 = (bf16[400,128]{1,0:T(8,128)(2,1)S(1)}, bf16[400,128]{1,0:T(8,128)(2,1)S(1)}, u32[]{:S(2)}, u32[]{:S(2)}) collective-permute-start(bf16[400,128]{1,0:T(8,128)(2,1)S(1)} %get-tuple-element.5234), channel_id=1, source_target_pairs={{8,7},{24,23},{40,39},{56,55},{72,71},{88,87},{104,103},{120,119}} | collective-permute-start | bytes 307208 | tf_op jit(solution)/shard_map/while/body/eval_jaxpr/ppermute | solution.py:32
  586.2 14.9 %collective-permute-start.35 = (bf16[400,128]{1,0:T(8,128)(2,1)S(1)}, bf16[400,128]{1,0:T(8,128)(2,1)S(1)}, u32[]{:S(2)}, u32[]{:S(2)}) collective-permute-start(bf16[400,128]{1,0:T(8,128)(2,1)S(1)} %get-tuple-element.5234), channel_id=1, source_target_pairs={{8,7},{24,23},{40,39},{56,55},{72,71},{88,87},{104,103},{120,119}} | collective-permute-start | bytes 307208 | tf_op jit(solution)/shard_map/while/body/eval_jaxpr/ppermute | solution.py:32
  609.8 14.8 %collective-permute-start.35 = (bf16[400,128]{1,0:T(8,128)(2,1)S(1)}, bf16[400,128]{1,0:T(8,128)(2,1)S(1)}, u32[]{:S(2)}, u32[]{:S(2)}) collective-permute-start(bf16[400,128]{1,0:T(8,128)(2,1)S(1)} %get-tuple-element.5234), channel_id=1, source_target_pairs={{8,7},{24,23},{40,39},{56,55},{72,71},{88,87},{104,103},{120,119}} | collective-permute-start | bytes 307208 | tf_op jit(solution)/shard_map/while/body/eval_jaxpr/ppermute | solution.py:32
  634.6 14.9 %collective-permute-start.35 = (bf16[400,128]{1,0:T(8,128)(2,1)S(1)}, bf16[400,128]{1,0:T(8,128)(2,1)S(1)}, u32[]{:S(2)}, u32[]{:S(2)}) collective-permute-start(bf16[400,128]{1,0:T(8,128)(2,1)S(1)} %get-tuple-element.5234), channel_id=1, source_target_pairs={{8,7},{24,23},{40,39},{56,55},{72,71},{88,87},{104,103},{120,119}} | collective-permute-start | bytes 307208 | tf_op jit(solution)/shard_map/while/body/eval_jaxpr/ppermute | solution.py:32
  658.1 14.8 %collective-permute-start.35 = (bf16[400,128]{1,0:T(8,128)(2,1)S(1)}, bf16[400,128]{1,0:T(8,128)(2,1)S(1)}, u32[]{:S(2)}, u32[]{:S(2)}) collective-permute-start(bf16[400,128]{1,0:T(8,128)(2,1)S(1)} %get-tuple-element.5234), channel_id=1, source_target_pairs={{8,7},{24,23},{40,39},{56,55},{72,71},{88,87},{104,103},{120,119}} | collective-permute-start | bytes 307208 | tf_op jit(solution)/shard_map/while/body/eval_jaxpr/ppermute | solution.py:32
  682.9 14.9 %collective-permute-start.35 = (bf16[400,128]{1,0:T(8,128)(2,1)S(1)}, bf16[400,128]{1,0:T(8,128)(2,1)S(1)}, u32[]{:S(2)}, u32[]{:S(2)}) collective-permute-start(bf16[400,128]{1,0:T(8,128)(2,1)S(1)} %get-tuple-element.5234), channel_id=1, source_target_pairs={{8,7},{24,23},{40,39},{56,55},{72,71},{88,87},{104,103},{120,119}} | collective-permute-start | bytes 307208 | tf_op jit(solution)/shard_map/while/body/eval_jaxpr/ppermute | solution.py:32
  706.5 14.8 %collective-permute-start.35 = (bf16[400,128]{1,0:T(8,128)(2,1)S(1)}, bf16[400,128]{1,0:T(8,128)(2,1)S(1)}, u32[]{:S(2)}, u32[]{:S(2)}) collective-permute-start(bf16[400,128]{1,0:T(8,128)(2,1)S(1)} %get-tuple-element.5234), channel_id=1, source_target_pairs={{8,7},{24,23},{40,39},{56,55},{72,71},{88,87},{104,103},{120,119}} | collective-permute-start | bytes 307208 | tf_op jit(solution)/shard_map/while/body/eval_jaxpr/ppermute | solution.py:32
  731.2 15.0 %collective-permute-start.35 = (bf16[400,128]{1,0:T(8,128)(2,1)S(1)}, bf16[400,128]{1,0:T(8,128)(2,1)S(1)}, u32[]{:S(2)}, u32[]{:S(2)}) collective-permute-start(bf16[400,128]{1,0:T(8,128)(2,1)S(1)} %get-tuple-element.5234), channel_id=1, source_target_pairs={{8,7},{24,23},{40,39},{56,55},{72,71},{88,87},{104,103},{120,119}} | collective-permute-start | bytes 307208 | tf_op jit(solution)/shard_map/while/body/eval_jaxpr/ppermute | solution.py:32
  754.9 14.8 %collective-permute-start.35 = (bf16[400,128]{1,0:T(8,128)(2,1)S(1)}, bf16[400,128]{1,0:T(8,128)(2,1)S(1)}, u32[]{:S(2)}, u32[]{:S(2)}) collective-permute-start(bf16[400,128]{1,0:T(8,128)(2,1)S(1)} %get-tuple-element.5234), channel_id=1, source_target_pairs={{8,7},{24,23},{40,39},{56,55},{72,71},{88,87},{104,103},{120,119}} | collective-permute-start | bytes 307208 | tf_op jit(solution)/shard_map/while/body/eval_jaxpr/ppermute | solution.py:32
  779.6 15.0 %collective-permute-start.35 = (bf16[400,128]{1,0:T(8,128)(2,1)S(1)}, bf16[400,128]{1,0:T(8,128)(2,1)S(1)}, u32[]{:S(2)}, u32[]{:S(2)}) collective-permute-start(bf16[400,128]{1,0:T(8,128)(2,1)S(1)} %get-tuple-element.5234), channel_id=1, source_target_pairs={{8,7},{24,23},{40,39},{56,55},{72,71},{88,87},{104,103},{120,119}} | collective-permute-start | bytes 307208 | tf_op jit(solution)/shard_map/while/body/eval_jaxpr/ppermute | solution.py:32
  803.2 14.8 %collective-permute-start.35 = (bf16[400,128]{1,0:T(8,128)(2,1)S(1)}, bf16[400,128]{1,0:T(8,128)(2,1)S(1)}, u32[]{:S(2)}, u32[]{:S(2)}) collective-permute-start(bf16[400,128]{1,0:T(8,128)(2,1)S(1)} %get-tuple-element.5234), channel_id=1, source_target_pairs={{8,7},{24,23},{40,39},{56,55},{72,71},{88,87},{104,103},{120,119}} | collective-permute-start | bytes 307208 | tf_op jit(solution)/shard_map/while/body/eval_jaxpr/ppermute | solution.py:32
  828.0 14.9 %collective-permute-start.35 = (bf16[400,128]{1,0:T(8,128)(2,1)S(1)}, bf16[400,128]{1,0:T(8,128)(2,1)S(1)}, u32[]{:S(2)}, u32[]{:S(2)}) collective-permute-start(bf16[400,128]{1,0:T(8,128)(2,1)S(1)} %get-tuple-element.5234), channel_id=1, source_target_pairs={{8,7},{24,23},{40,39},{56,55},{72,71},{88,87},{104,103},{120,119}} | collective-permute-start | bytes 307208 | tf_op jit(solution)/shard_map/while/body/eval_jaxpr/ppermute | solution.py:32
  851.6 14.8 %collective-permute-start.35 = (bf16[400,128]{1,0:T(8,128)(2,1)S(1)}, bf16[400,128]{1,0:T(8,128)(2,1)S(1)}, u32[]{:S(2)}, u32[]{:S(2)}) collective-permute-start(bf16[400,128]{1,0:T(8,128)(2,1)S(1)} %get-tuple-element.5234), channel_id=1, source_target_pairs={{8,7},{24,23},{40,39},{56,55},{72,71},{88,87},{104,103},{120,119}} | collective-permute-start | bytes 307208 | tf_op jit(solution)/shard_map/while/body/eval_jaxpr/ppermute | solution.py:32
  876.3 14.9 %collective-permute-start.35 = (bf16[400,128]{1,0:T(8,128)(2,1)S(1)}, bf16[400,128]{1,0:T(8,128)(2,1)S(1)}, u32[]{:S(2)}, u32[]{:S(2)}) collective-permute-start(bf16[400,128]{1,0:T(8,128)(2,1)S(1)} %get-tuple-element.5234), channel_id=1, source_target_pairs={{8,7},{24,23},{40,39},{56,55},{72,71},{88,87},{104,103},{120,119}} | collective-permute-start | bytes 307208 | tf_op jit(solution)/shard_map/while/body/eval_jaxpr/ppermute | solution.py:32
  899.9 14.8 %collective-permute-start.35 = (bf16[400,128]{1,0:T(8,128)(2,1)S(1)}, bf16[400,128]{1,0:T(8,128)(2,1)S(1)}, u32[]{:S(2)}, u32[]{:S(2)}) collective-permute-start(bf16[400,128]{1,0:T(8,128)(2,1)S(1)} %get-tuple-element.5234), channel_id=1, source_target_pairs={{8,7},{24,23},{40,39},{56,55},{72,71},{88,87},{104,103},{120,119}} | collective-permute-start | bytes 307208 | tf_op jit(solution)/shard_map/while/body/eval_jaxpr/ppermute | solution.py:32
  924.6 14.9 %collective-permute-start.35 = (bf16[400,128]{1,0:T(8,128)(2,1)S(1)}, bf16[400,128]{1,0:T(8,128)(2,1)S(1)}, u32[]{:S(2)}, u32[]{:S(2)}) collective-permute-start(bf16[400,128]{1,0:T(8,128)(2,1)S(1)} %get-tuple-element.5234), channel_id=1, source_target_pairs={{8,7},{24,23},{40,39},{56,55},{72,71},{88,87},{104,103},{120,119}} | collective-permute-start | bytes 307208 | tf_op jit(solution)/shard_map/while/body/eval_jaxpr/ppermute | solution.py:32
  948.2 14.8 %collective-permute-start.35 = (bf16[400,128]{1,0:T(8,128)(2,1)S(1)}, bf16[400,128]{1,0:T(8,128)(2,1)S(1)}, u32[]{:S(2)}, u32[]{:S(2)}) collective-permute-start(bf16[400,128]{1,0:T(8,128)(2,1)S(1)} %get-tuple-element.5234), channel_id=1, source_target_pairs={{8,7},{24,23},{40,39},{56,55},{72,71},{88,87},{104,103},{120,119}} | collective-permute-start | bytes 307208 | tf_op jit(solution)/shard_map/while/body/eval_jaxpr/ppermute | solution.py:32
  972.9 14.9 %collective-permute-start.35 = (bf16[400,128]{1,0:T(8,128)(2,1)S(1)}, bf16[400,128]{1,0:T(8,128)(2,1)S(1)}, u32[]{:S(2)}, u32[]{:S(2)}) collective-permute-start(bf16[400,128]{1,0:T(8,128)(2,1)S(1)} %get-tuple-element.5234), channel_id=1, source_target_pairs={{8,7},{24,23},{40,39},{56,55},{72,71},{88,87},{104,103},{120,119}} | collective-permute-start | bytes 307208 | tf_op jit(solution)/shard_map/while/body/eval_jaxpr/ppermute | solution.py:32
  1006.4 20.6 %collective-permute-start.52 = (bf16[16,192,128]{2,1,0:T(8,128)(2,1)S(1)}, bf16[16,192,128]{2,1,0:T(8,128)(2,1)S(1)}, u32[]{:S(2)}, u32[]{:S(2)}) collective-permute-start(bf16[16,192,128]{2,1,0:T(8,128)(2,1)S(1)} %get-tuple-element.4045), channel_id=1, source_target_pairs={{0,1},{16,19},{32,37},{48,55},{64,73},{80,91},{96,109},{112,127}} | collective-permute-start | bytes 2359304 | tf_op jit(solution)/shard_map/ppermute | solution.py:460
  1007.1 19.9 %collective-permute-start.53 = (bf16[16,192,128]{2,1,0:T(8,128)(2,1)S(1)}, bf16[16,192,128]{2,1,0:T(8,128)(2,1)S(1)}, u32[]{:S(2)}, u32[]{:S(2)}) collective-permute-start(bf16[16,192,128]{2,1,0:T(8,128)(2,1)S(1)} %get-tuple-element.4044), channel_id=1, source_target_pairs={{0,0},{16,18},{32,36},{48,54},{64,72},{80,90},{96,108},{112,126}} | collective-permute-start | bytes 2359304 | tf_op jit(solution)/shard_map/ppermute | solution.py:460
  1028.2 18.8 %all-to-all-start.2 = ((bf16[8,16,8,384]{3,2,1,0:T(8,128)(2,1)}), bf16[8,16,8,384]{3,2,1,0:T(8,128)(2,1)S(1)}, u32[]{:S(2)}, u32[]{:S(2)}) async-start(bf16[8,16,8,384]{3,2,1,0:T(8,128)(2,1)} %bitcast.181), calls=%async_computation.2 | async-start | bytes 1572864 | tf_op jit(solution)/shard_map/all_to_all | solution.py:468
  (272 other events, 2072.9 us)
Sparse Core Ops, SparseCore 0:
  20.9 105.9 all-gather.4
  128.6 56.0 all-gather.6
  186.3 48.1 all-gather.8
  236.1 65.3 all-gather.10
